TPU v7x, 256 devices: a whole 4x4x8 slice. The times are simulated.
256 devices in a mesh: ta: 16 (over z_lo, y, core), gz: 16 (over x, z_hi).
Axes of the slice: x: 4, y: 4, z: 8 (z_hi: 4, z_lo: 2; z = z_hi * 2 + z_lo), core: 2. Of those that a mesh axis runs over, the one named last changes fastest.
Arguments:
- source: bfloat16 [16, 16, 16, 96, 128], P('ta', 'gz'), may hold values from -6 to 6
- link_blocks: bfloat16 [16, 16, 16, 9, 96, 96], P('ta', 'gz'), may hold values from -0.21875 to 0.21875
Outputs:
- result: float32 [16, 16, 16, 96, 128], P('ta', 'gz')
All inputs are finite; a program needn't handle non-finite values.
Results may differ from a plain program's by a relative error of at most 0.0049.
Values may be sent and summed in bfloat16 or wider, within the bound.
A program may use at most 64 MiB of HBM per device.

v0:
```python
import jax
import jax.numpy as jnp
from jax import lax
from jax.sharding import PartitionSpec as P

DOF = 96
DIRS = 9
NX = 8
NY = 2
APPLIES = 4


def shifted(block, axis, distance):
    devices = range(lax.axis_size(axis))
    route = [((i - distance) % len(devices), i) for i in devices]
    return lax.ppermute(block, axis, route)


def padded(value, sides, width):
    for axis, dim in sides:
        size, length = (lax.axis_size(axis), value.shape[dim])
        up = [(i, (i + 1) % size) for i in range(size)]
        down = [(j, i) for i, j in up]
        last = lax.slice_in_dim(value, length - width, length, axis=dim)
        first = lax.slice_in_dim(value, 0, width, axis=dim)
        before = lax.ppermute(last, axis, up)
        after = lax.ppermute(first, axis, down)
        value = jnp.concatenate([before, value, after], axis=dim)
    return value


def apply_operator(vectors, coupling):
    slices = vectors.shape[0]
    depth = vectors.shape[1]
    sites = vectors.shape[2]
    from_below = shifted(vectors, "ta", 1)
    from_above = shifted(vectors, "ta", -1)
    z_padded = padded(vectors, (("gz", 1),), 1)
    z_after = z_padded[:, 2:]
    z_before = z_padded[:, :-2]
    t_after = jnp.concatenate([vectors[1:], from_above], 0)
    t_before = jnp.concatenate([from_below, vectors[:-1]], 0)
    row_count = DOF
    col_count = vectors.shape[4]
    planes = vectors.reshape(slices, depth, NY, NX, row_count, col_count)
    neighbours = [
        vectors,
        jnp.roll(planes, -1, axis=3).reshape(slices, depth, sites, row_count, col_count),
        jnp.roll(planes, 1, axis=3).reshape(slices, depth, sites, row_count, col_count),
        jnp.roll(planes, -1, axis=2).reshape(slices, depth, sites, row_count, col_count),
        jnp.roll(planes, 1, axis=2).reshape(slices, depth, sites, row_count, col_count),
        z_after,
        z_before,
        t_after,
        t_before,
    ]
    summed = jnp.zeros((slices, depth, sites, row_count, col_count), jnp.float32)
    for direction in range(DIRS):
        summed = summed + jnp.einsum(
            "tzsab,tzsbr->tzsar",
            coupling[:, :, :, direction],
            neighbours[direction],
            preferred_element_type=jnp.float32,
        )
    return summed


def shards(source, link_blocks):
    summed = apply_operator(source, link_blocks)
    for apply_step in range(APPLIES - 1):
        summed = apply_operator(summed.astype(jnp.bfloat16), link_blocks)
    return summed


def solution(mesh):
    placed = (P("ta", "gz", None, None, None), P("ta", "gz", None, None, None, None))
    return jax.shard_map(
        shards,
        mesh=mesh,
        in_specs=placed,
        out_specs=P("ta", "gz", None, None, None),
        check_vma=False,
    )
```

profile of v0, /device:TPU:25, one launch (start us, length us, event | category | flops | bytes accessed | tf_op | source)
XLA Modules:
  0.0 116.6 jit_solution(2496894800308951840)
XLA Ops:
  0.0 1.9 %collective-permute-start.3 = (bf16[1,1,16,96,128]{4,3,2,1,0:T(8,128)(2,1)}, bf16[1,1,16,96,128]{4,3,2,1,0:T(8,128)(2,1)S(1)}, u32[]{:S(2)}, u32[]{:S(2)}) collective-permute-start(bf16[1,1,16,96,128]{4,3,2,1,0:T(8,128)(2,1)} %param.2), channel_id=1, source_target_pairs={{240,0},{0,16},{16,32},{32,48},{48,64},{64,80},{80,96},{96,112},{1... | collective-permute-start | bytes 1179656 | tf_op jit(solution)/shard_map/ppermute | solution.py:16
  1.9 3.0 %collective-permute-start.1 = (bf16[1,1,16,96,128]{4,3,2,1,0:T(8,128)(2,1)}, bf16[1,1,16,96,128]{4,3,2,1,0:T(8,128)(2,1)S(1)}, u32[]{:S(2)}, u32[]{:S(2)}) collective-permute-start(bf16[1,1,16,96,128]{4,3,2,1,0:T(8,128)(2,1)} %param.2), channel_id=1, source_target_pairs={{0,1},{1,2},{2,3},{3,4},{4,5},{5,6},{6,7},{7,8},{8,9},{9,10},{10,1... | collective-permute-start | bytes 1179656 | tf_op jit(solution)/shard_map/ppermute | solution.py:26
  4.9 4.3 %collective-permute-start = (bf16[1,1,16,96,128]{4,3,2,1,0:T(8,128)(2,1)}, bf16[1,1,16,96,128]{4,3,2,1,0:T(8,128)(2,1)S(1)}, u32[]{:S(2)}, u32[]{:S(2)}) collective-permute-start(bf16[1,1,16,96,128]{4,3,2,1,0:T(8,128)(2,1)} %param.2), channel_id=1, source_target_pairs={{1,0},{2,1},{3,2},{4,3},{5,4},{6,5},{7,6},{8,7},{9,8},{10,9},{11,1... | collective-permute-start | bytes 1179656 | tf_op jit(solution)/shard_map/ppermute | solution.py:27
  9.2 1.1 fusion.134
  10.3 0.8 fusion.133
  11.2 1.0 fusion.132
  12.6 0.3 convolution_add_fusion.16
  12.8 0.3 fusion.2
  13.1 0.3 fusion.1
  13.4 0.3 fusion
  13.9 6.9 %collective-permute-done.2 = bf16[1,1,16,96,128]{4,3,2,1,0:T(8,128)(2,1)S(1)} collective-permute-done((bf16[1,1,16,96,128]{4,3,2,1,0:T(8,128)(2,1)}, bf16[1,1,16,96,128]{4,3,2,1,0:T(8,128)(2,1)S(1)}, u32[]{:S(2)}, u32[]{:S(2)}) %collective-permute-start.2) | collective-permute-done | bytes 393248 | tf_op jit(solution)/shard_map/ppermute | solution.py:16
  21.1 10.3 %collective-permute-done.1 = bf16[1,1,16,96,128]{4,3,2,1,0:T(8,128)(2,1)S(1)} collective-permute-done((bf16[1,1,16,96,128]{4,3,2,1,0:T(8,128)(2,1)}, bf16[1,1,16,96,128]{4,3,2,1,0:T(8,128)(2,1)S(1)}, u32[]{:S(2)}, u32[]{:S(2)}) %collective-permute-start.1) | collective-permute-done | bytes 393248 | tf_op jit(solution)/shard_map/ppermute | solution.py:26
  31.7 0.3 fusion.18
  32.6 0.4 collective-permute-start.6
  33.0 2.9 %collective-permute-start.5 = (bf16[1,1,16,96,128]{4,3,2,1,0:T(8,128)(2,1)S(1)}, bf16[1,1,16,96,128]{4,3,2,1,0:T(8,128)(2,1)S(1)}, u32[]{:S(2)}, u32[]{:S(2)}) collective-permute-start(bf16[1,1,16,96,128]{4,3,2,1,0:T(8,128)(2,1)S(1)} %bitcast.217), channel_id=1, source_target_pairs={{0,1},{1,2},{2,3},{3,4},{4,5},{5,6},{6,7},{7,8},{8,9},{9,10},{10,1... | collective-permute-start | bytes 1179656 | tf_op jit(solution)/shard_map/ppermute | solution.py:26
  35.9 2.8 %collective-permute-start.4 = (bf16[1,1,16,96,128]{4,3,2,1,0:T(8,128)(2,1)S(1)}, bf16[1,1,16,96,128]{4,3,2,1,0:T(8,128)(2,1)S(1)}, u32[]{:S(2)}, u32[]{:S(2)}) collective-permute-start(bf16[1,1,16,96,128]{4,3,2,1,0:T(8,128)(2,1)S(1)} %bitcast.218), channel_id=1, source_target_pairs={{1,0},{2,1},{3,2},{4,3},{5,4},{6,5},{7,6},{8,7},{9,8},{10,9},{11,1... | collective-permute-start | bytes 1179656 | tf_op jit(solution)/shard_map/ppermute | solution.py:27
  38.7 0.3 convolution_add_fusion.14
  39.0 0.3 convolution_add_fusion.13
  39.3 0.3 convolution_add_fusion.12
  39.8 9.6 %collective-permute-done.7 = bf16[1,1,16,96,128]{4,3,2,1,0:T(8,128)(2,1)S(1)} collective-permute-done((bf16[1,1,16,96,128]{4,3,2,1,0:T(8,128)(2,1)S(1)}, bf16[1,1,16,96,128]{4,3,2,1,0:T(8,128)(2,1)S(1)}, u32[]{:S(2)}, u32[]{:S(2)}) %collective-permute-start.7) | collective-permute-done | bytes 393248 | tf_op jit(solution)/shard_map/ppermute | solution.py:16
  49.7 4.4 %collective-permute-done.6 = bf16[1,1,16,96,128]{4,3,2,1,0:T(8,128)(2,1)S(1)} collective-permute-done((bf16[1,1,16,96,128]{4,3,2,1,0:T(8,128)(2,1)S(1)}, bf16[1,1,16,96,128]{4,3,2,1,0:T(8,128)(2,1)S(1)}, u32[]{:S(2)}, u32[]{:S(2)}) %collective-permute-start.6) | collective-permute-done | bytes 393248 | tf_op jit(solution)/shard_map/ppermute | solution.py:16
  54.3 3.5 %collective-permute-done.5 = bf16[1,1,16,96,128]{4,3,2,1,0:T(8,128)(2,1)S(1)} collective-permute-done((bf16[1,1,16,96,128]{4,3,2,1,0:T(8,128)(2,1)S(1)}, bf16[1,1,16,96,128]{4,3,2,1,0:T(8,128)(2,1)S(1)}, u32[]{:S(2)}, u32[]{:S(2)}) %collective-permute-start.5) | collective-permute-done | bytes 393248 | tf_op jit(solution)/shard_map/ppermute | solution.py:26
  58.1 0.3 fusion.17
  58.8 3.0 %collective-permute-start.11 = (bf16[1,1,16,96,128]{4,3,2,1,0:T(8,128)(2,1)S(1)}, bf16[1,1,16,96,128]{4,3,2,1,0:T(8,128)(2,1)S(1)}, u32[]{:S(2)}, u32[]{:S(2)}) collective-permute-start(bf16[1,1,16,96,128]{4,3,2,1,0:T(8,128)(2,1)S(1)} %bitcast.222), channel_id=1, source_target_pairs={{240,0},{0,16},{16,32},{32,48},{48,64},{64,80},{80,96},{96,112},{1... | collective-permute-start | bytes 1179656 | tf_op jit(solution)/shard_map/ppermute | solution.py:16
  61.8 1.2 %collective-permute-start.9 = (bf16[1,1,16,96,128]{4,3,2,1,0:T(8,128)(2,1)S(1)}, bf16[1,1,16,96,128]{4,3,2,1,0:T(8,128)(2,1)S(1)}, u32[]{:S(2)}, u32[]{:S(2)}) collective-permute-start(bf16[1,1,16,96,128]{4,3,2,1,0:T(8,128)(2,1)S(1)} %bitcast.224), channel_id=1, source_target_pairs={{0,1},{1,2},{2,3},{3,4},{4,5},{5,6},{6,7},{7,8},{8,9},{9,10},{10,1... | collective-permute-start | bytes 1179656 | tf_op jit(solution)/shard_map/ppermute | solution.py:26
  63.0 4.5 %collective-permute-start.8 = (bf16[1,1,16,96,128]{4,3,2,1,0:T(8,128)(2,1)S(1)}, bf16[1,1,16,96,128]{4,3,2,1,0:T(8,128)(2,1)S(1)}, u32[]{:S(2)}, u32[]{:S(2)}) collective-permute-start(bf16[1,1,16,96,128]{4,3,2,1,0:T(8,128)(2,1)S(1)} %bitcast.225), channel_id=1, source_target_pairs={{1,0},{2,1},{3,2},{4,3},{5,4},{6,5},{7,6},{8,7},{9,8},{10,9},{11,1... | collective-permute-start | bytes 1179656 | tf_op jit(solution)/shard_map/ppermute | solution.py:27
  67.6 0.3 convolution_add_fusion.9
  67.9 0.3 convolution_add_fusion.8
  68.1 0.3 convolution_add_fusion.7
  68.4 0.3 convolution_add_fusion.6
  68.6 8.3 %collective-permute-done.11 = bf16[1,1,16,96,128]{4,3,2,1,0:T(8,128)(2,1)S(1)} collective-permute-done((bf16[1,1,16,96,128]{4,3,2,1,0:T(8,128)(2,1)S(1)}, bf16[1,1,16,96,128]{4,3,2,1,0:T(8,128)(2,1)S(1)}, u32[]{:S(2)}, u32[]{:S(2)}) %collective-permute-start.11) | collective-permute-done | bytes 393248 | tf_op jit(solution)/shard_map/ppermute | solution.py:16
  76.9 0.3 fusion.21
  77.2 6.1 %collective-permute-done.10 = bf16[1,1,16,96,128]{4,3,2,1,0:T(8,128)(2,1)S(1)} collective-permute-done((bf16[1,1,16,96,128]{4,3,2,1,0:T(8,128)(2,1)S(1)}, bf16[1,1,16,96,128]{4,3,2,1,0:T(8,128)(2,1)S(1)}, u32[]{:S(2)}, u32[]{:S(2)}) %collective-permute-start.10) | collective-permute-done | bytes 393248 | tf_op jit(solution)/shard_map/ppermute | solution.py:16
  83.5 3.6 %collective-permute-done.9 = bf16[1,1,16,96,128]{4,3,2,1,0:T(8,128)(2,1)S(1)} collective-permute-done((bf16[1,1,16,96,128]{4,3,2,1,0:T(8,128)(2,1)S(1)}, bf16[1,1,16,96,128]{4,3,2,1,0:T(8,128)(2,1)S(1)}, u32[]{:S(2)}, u32[]{:S(2)}) %collective-permute-start.9) | collective-permute-done | bytes 393248 | tf_op jit(solution)/shard_map/ppermute | solution.py:26
  87.4 0.3 fusion.16
  88.1 0.8 collective-permute-start.15
  88.9 0.5 collective-permute-start.13
  89.4 5.2 %collective-permute-start.12 = (bf16[1,1,16,96,128]{4,3,2,1,0:T(8,128)(2,1)S(1)}, bf16[1,1,16,96,128]{4,3,2,1,0:T(8,128)(2,1)S(1)}, u32[]{:S(2)}, u32[]{:S(2)}) collective-permute-start(bf16[1,1,16,96,128]{4,3,2,1,0:T(8,128)(2,1)S(1)} %bitcast.232), channel_id=1, source_target_pairs={{1,0},{2,1},{3,2},{4,3},{5,4},{6,5},{7,6},{8,7},{9,8},{10,9},{11,1... | collective-permute-start | bytes 1179656 | tf_op jit(solution)/shard_map/ppermute | solution.py:27
  94.8 0.3 convolution_add_fusion.4
  95.0 0.3 convolution_add_fusion.3
  95.3 0.3 convolution_add_fusion.2
  95.5 0.3 convolution_add_fusion.1
  95.8 8.8 %collective-permute-done.15 = bf16[1,1,16,96,128]{4,3,2,1,0:T(8,128)(2,1)S(1)} collective-permute-done((bf16[1,1,16,96,128]{4,3,2,1,0:T(8,128)(2,1)S(1)}, bf16[1,1,16,96,128]{4,3,2,1,0:T(8,128)(2,1)S(1)}, u32[]{:S(2)}, u32[]{:S(2)}) %collective-permute-start.15) | collective-permute-done | bytes 393248 | tf_op jit(solution)/shard_map/ppermute | solution.py:16
  104.8 6.1 %collective-permute-done.14 = bf16[1,1,16,96,128]{4,3,2,1,0:T(8,128)(2,1)S(1)} collective-permute-done((bf16[1,1,16,96,128]{4,3,2,1,0:T(8,128)(2,1)S(1)}, bf16[1,1,16,96,128]{4,3,2,1,0:T(8,128)(2,1)S(1)}, u32[]{:S(2)}, u32[]{:S(2)}) %collective-permute-start.14) | collective-permute-done | bytes 393248 | tf_op jit(solution)/shard_map/ppermute | solution.py:16
  110.9 0.3 fusion.31
  111.2 3.9 %collective-permute-done.13 = bf16[1,1,16,96,128]{4,3,2,1,0:T(8,128)(2,1)S(1)} collective-permute-done((bf16[1,1,16,96,128]{4,3,2,1,0:T(8,128)(2,1)S(1)}, bf16[1,1,16,96,128]{4,3,2,1,0:T(8,128)(2,1)S(1)}, u32[]{:S(2)}, u32[]{:S(2)}) %collective-permute-start.13) | collective-permute-done | bytes 393248 | tf_op jit(solution)/shard_map/ppermute | solution.py:26
  115.1 0.3 fusion.39
  115.4 1.2 fusion.15
  (47 shorter events, 4.5 us)
Async XLA Ops:
  0.0 12.6 %copy-start.1 = (bf16[1,1,16,96,128]{4,3,2,1,0:T(8,128)(2,1)S(1)}, bf16[1,1,16,96,128]{4,3,2,1,0:T(8,128)(2,1)}, u32[]{:S(2)}) copy-start(bf16[1,1,16,96,128]{4,3,2,1,0:T(8,128)(2,1)} %param.2) | copy-start | bytes 1179652
  0.0 12.3 %copy-start = (bf16[1,1,16,9,96,96]{5,4,3,2,1,0:T(8,128)(2,1)S(1)}, bf16[1,1,16,9,96,96]{5,4,3,2,1,0:T(8,128)(2,1)}, u32[]{:S(2)}) copy-start(bf16[1,1,16,9,96,96]{5,4,3,2,1,0:T(8,128)(2,1)} %param.3) | copy-start | bytes 7962628
  0.0 13.7 %collective-permute-start.3 = (bf16[1,1,16,96,128]{4,3,2,1,0:T(8,128)(2,1)}, bf16[1,1,16,96,128]{4,3,2,1,0:T(8,128)(2,1)S(1)}, u32[]{:S(2)}, u32[]{:S(2)}) collective-permute-start(bf16[1,1,16,96,128]{4,3,2,1,0:T(8,128)(2,1)} %param.2), channel_id=1, source_target_pairs={{240,0},{0,16},{16,32},{32,48},{48,64},{64,80},{80,96},{96,112},{1... | collective-permute-start | bytes 1179656 | tf_op jit(solution)/shard_map/ppermute | solution.py:16
  1.9 19.0 %collective-permute-start.2 = (bf16[1,1,16,96,128]{4,3,2,1,0:T(8,128)(2,1)}, bf16[1,1,16,96,128]{4,3,2,1,0:T(8,128)(2,1)S(1)}, u32[]{:S(2)}, u32[]{:S(2)}) collective-permute-start(bf16[1,1,16,96,128]{4,3,2,1,0:T(8,128)(2,1)} %param.2), channel_id=1, source_target_pairs={{16,0},{32,16},{48,32},{64,48},{80,64},{96,80},{112,96},{128,112},... | collective-permute-start | bytes 1179656 | tf_op jit(solution)/shard_map/ppermute | solution.py:16
  1.9 29.5 %collective-permute-start.1 = (bf16[1,1,16,96,128]{4,3,2,1,0:T(8,128)(2,1)}, bf16[1,1,16,96,128]{4,3,2,1,0:T(8,128)(2,1)S(1)}, u32[]{:S(2)}, u32[]{:S(2)}) collective-permute-start(bf16[1,1,16,96,128]{4,3,2,1,0:T(8,128)(2,1)} %param.2), channel_id=1, source_target_pairs={{0,1},{1,2},{2,3},{3,4},{4,5},{5,6},{6,7},{7,8},{8,9},{9,10},{10,1... | collective-permute-start | bytes 1179656 | tf_op jit(solution)/shard_map/ppermute | solution.py:26
  4.9 26.8 %collective-permute-start = (bf16[1,1,16,96,128]{4,3,2,1,0:T(8,128)(2,1)}, bf16[1,1,16,96,128]{4,3,2,1,0:T(8,128)(2,1)S(1)}, u32[]{:S(2)}, u32[]{:S(2)}) collective-permute-start(bf16[1,1,16,96,128]{4,3,2,1,0:T(8,128)(2,1)} %param.2), channel_id=1, source_target_pairs={{1,0},{2,1},{3,2},{4,3},{5,4},{6,5},{7,6},{8,7},{9,8},{10,9},{11,1... | collective-permute-start | bytes 1179656 | tf_op jit(solution)/shard_map/ppermute | solution.py:27
  32.4 17.1 %collective-permute-start.7 = (bf16[1,1,16,96,128]{4,3,2,1,0:T(8,128)(2,1)S(1)}, bf16[1,1,16,96,128]{4,3,2,1,0:T(8,128)(2,1)S(1)}, u32[]{:S(2)}, u32[]{:S(2)}) collective-permute-start(bf16[1,1,16,96,128]{4,3,2,1,0:T(8,128)(2,1)S(1)} %bitcast.215), channel_id=1, source_target_pairs={{240,0},{0,16},{16,32},{32,48},{48,64},{64,80},{80,96},{96,112},{1... | collective-permute-start | bytes 1179656 | tf_op jit(solution)/shard_map/ppermute | solution.py:16
  32.6 21.5 %collective-permute-start.6 = (bf16[1,1,16,96,128]{4,3,2,1,0:T(8,128)(2,1)S(1)}, bf16[1,1,16,96,128]{4,3,2,1,0:T(8,128)(2,1)S(1)}, u32[]{:S(2)}, u32[]{:S(2)}) collective-permute-start(bf16[1,1,16,96,128]{4,3,2,1,0:T(8,128)(2,1)S(1)} %bitcast.216), channel_id=1, source_target_pairs={{16,0},{32,16},{48,32},{64,48},{80,64},{96,80},{112,96},{128,112},... | collective-permute-start | bytes 1179656 | tf_op jit(solution)/shard_map/ppermute | solution.py:16
  33.0 24.9 %collective-permute-start.5 = (bf16[1,1,16,96,128]{4,3,2,1,0:T(8,128)(2,1)S(1)}, bf16[1,1,16,96,128]{4,3,2,1,0:T(8,128)(2,1)S(1)}, u32[]{:S(2)}, u32[]{:S(2)}) collective-permute-start(bf16[1,1,16,96,128]{4,3,2,1,0:T(8,128)(2,1)S(1)} %bitcast.217), channel_id=1, source_target_pairs={{0,1},{1,2},{2,3},{3,4},{4,5},{5,6},{6,7},{7,8},{8,9},{9,10},{10,1... | collective-permute-start | bytes 1179656 | tf_op jit(solution)/shard_map/ppermute | solution.py:26
  35.9 22.2 %collective-permute-start.4 = (bf16[1,1,16,96,128]{4,3,2,1,0:T(8,128)(2,1)S(1)}, bf16[1,1,16,96,128]{4,3,2,1,0:T(8,128)(2,1)S(1)}, u32[]{:S(2)}, u32[]{:S(2)}) collective-permute-start(bf16[1,1,16,96,128]{4,3,2,1,0:T(8,128)(2,1)S(1)} %bitcast.218), channel_id=1, source_target_pairs={{1,0},{2,1},{3,2},{4,3},{5,4},{6,5},{7,6},{8,7},{9,8},{10,9},{11,1... | collective-permute-start | bytes 1179656 | tf_op jit(solution)/shard_map/ppermute | solution.py:27
  58.8 18.2 %collective-permute-start.11 = (bf16[1,1,16,96,128]{4,3,2,1,0:T(8,128)(2,1)S(1)}, bf16[1,1,16,96,128]{4,3,2,1,0:T(8,128)(2,1)S(1)}, u32[]{:S(2)}, u32[]{:S(2)}) collective-permute-start(bf16[1,1,16,96,128]{4,3,2,1,0:T(8,128)(2,1)S(1)} %bitcast.222), channel_id=1, source_target_pairs={{240,0},{0,16},{16,32},{32,48},{48,64},{64,80},{80,96},{96,112},{1... | collective-permute-start | bytes 1179656 | tf_op jit(solution)/shard_map/ppermute | solution.py:16
  61.8 21.5 %collective-permute-start.10 = (bf16[1,1,16,96,128]{4,3,2,1,0:T(8,128)(2,1)S(1)}, bf16[1,1,16,96,128]{4,3,2,1,0:T(8,128)(2,1)S(1)}, u32[]{:S(2)}, u32[]{:S(2)}) collective-permute-start(bf16[1,1,16,96,128]{4,3,2,1,0:T(8,128)(2,1)S(1)} %bitcast.223), channel_id=1, source_target_pairs={{16,0},{32,16},{48,32},{64,48},{80,64},{96,80},{112,96},{128,112},... | collective-permute-start | bytes 1179656 | tf_op jit(solution)/shard_map/ppermute | solution.py:16
  61.8 25.4 %collective-permute-start.9 = (bf16[1,1,16,96,128]{4,3,2,1,0:T(8,128)(2,1)S(1)}, bf16[1,1,16,96,128]{4,3,2,1,0:T(8,128)(2,1)S(1)}, u32[]{:S(2)}, u32[]{:S(2)}) collective-permute-start(bf16[1,1,16,96,128]{4,3,2,1,0:T(8,128)(2,1)S(1)} %bitcast.224), channel_id=1, source_target_pairs={{0,1},{1,2},{2,3},{3,4},{4,5},{5,6},{6,7},{7,8},{8,9},{9,10},{10,1... | collective-permute-start | bytes 1179656 | tf_op jit(solution)/shard_map/ppermute | solution.py:26
  63.0 24.4 %collective-permute-start.8 = (bf16[1,1,16,96,128]{4,3,2,1,0:T(8,128)(2,1)S(1)}, bf16[1,1,16,96,128]{4,3,2,1,0:T(8,128)(2,1)S(1)}, u32[]{:S(2)}, u32[]{:S(2)}) collective-permute-start(bf16[1,1,16,96,128]{4,3,2,1,0:T(8,128)(2,1)S(1)} %bitcast.225), channel_id=1, source_target_pairs={{1,0},{2,1},{3,2},{4,3},{5,4},{6,5},{7,6},{8,7},{9,8},{10,9},{11,1... | collective-permute-start | bytes 1179656 | tf_op jit(solution)/shard_map/ppermute | solution.py:27
  88.1 16.5 %collective-permute-start.15 = (bf16[1,1,16,96,128]{4,3,2,1,0:T(8,128)(2,1)S(1)}, bf16[1,1,16,96,128]{4,3,2,1,0:T(8,128)(2,1)S(1)}, u32[]{:S(2)}, u32[]{:S(2)}) collective-permute-start(bf16[1,1,16,96,128]{4,3,2,1,0:T(8,128)(2,1)S(1)} %bitcast.229), channel_id=1, source_target_pairs={{240,0},{0,16},{16,32},{32,48},{48,64},{64,80},{80,96},{96,112},{1... | collective-permute-start | bytes 1179656 | tf_op jit(solution)/shard_map/ppermute | solution.py:16
  88.9 22.0 %collective-permute-start.14 = (bf16[1,1,16,96,128]{4,3,2,1,0:T(8,128)(2,1)S(1)}, bf16[1,1,16,96,128]{4,3,2,1,0:T(8,128)(2,1)S(1)}, u32[]{:S(2)}, u32[]{:S(2)}) collective-permute-start(bf16[1,1,16,96,128]{4,3,2,1,0:T(8,128)(2,1)S(1)} %bitcast.230), channel_id=1, source_target_pairs={{16,0},{32,16},{48,32},{64,48},{80,64},{96,80},{112,96},{128,112},... | collective-permute-start | bytes 1179656 | tf_op jit(solution)/shard_map/ppermute | solution.py:16
  88.9 26.2 %collective-permute-start.13 = (bf16[1,1,16,96,128]{4,3,2,1,0:T(8,128)(2,1)S(1)}, bf16[1,1,16,96,128]{4,3,2,1,0:T(8,128)(2,1)S(1)}, u32[]{:S(2)}, u32[]{:S(2)}) collective-permute-start(bf16[1,1,16,96,128]{4,3,2,1,0:T(8,128)(2,1)S(1)} %bitcast.231), channel_id=1, source_target_pairs={{0,1},{1,2},{2,3},{3,4},{4,5},{5,6},{6,7},{7,8},{8,9},{9,10},{10,1... | collective-permute-start | bytes 1179656 | tf_op jit(solution)/shard_map/ppermute | solution.py:26
  89.4 26.0 %collective-permute-start.12 = (bf16[1,1,16,96,128]{4,3,2,1,0:T(8,128)(2,1)S(1)}, bf16[1,1,16,96,128]{4,3,2,1,0:T(8,128)(2,1)S(1)}, u32[]{:S(2)}, u32[]{:S(2)}) collective-permute-start(bf16[1,1,16,96,128]{4,3,2,1,0:T(8,128)(2,1)S(1)} %bitcast.232), channel_id=1, source_target_pairs={{1,0},{2,1},{3,2},{4,3},{5,4},{6,5},{7,6},{8,7},{9,8},{10,9},{11,1... | collective-permute-start | bytes 1179656 | tf_op jit(solution)/shard_map/ppermute | solution.py:27
where the time goes:
time: 117 us
  waiting for transfers between devices  71.6 us (61%)
  starting transfers between devices  30.7 us (26%)
  matrix products  10 us (9%)
  local copies, waits for them, and re-layouts  3.41 us (3%)
    ppermute x8, waiting for transfers between devices, shifted(): return lax.ppermute(block, axis, route)  50.2 us
    ppermute x4, waiting for transfers between devices, padded(): before = lax.ppermute(last, axis, up)  21.4 us
    ppermute x4, starting transfers between devices, padded(): after = lax.ppermute(first, axis, down)  16.8 us
    dot_general x36, matrix products, apply_operator(): jnp.einsum('tzsab,tzsbr->tzsar', coupling[:, :, :, direction], neighbours...  10 us
    ppermute x4, starting transfers between devices, padded(): before = lax.ppermute(last, axis, up)  7.6 us
    ppermute x8, starting transfers between devices, shifted(): return lax.ppermute(block, axis, route)  6.3 us
  transfers between devices with their start and end apart: 16, of which 11 were waited for; matrix products, arithmetic and copies ran while one was open for 9% of the time, Pallas kernels for 0%

commit v1 on v0

v1 whole, which is shorter than its diff:
```python
import functools

import jax
import jax.numpy as jnp
from jax import lax
from jax.experimental import pallas as pl
from jax.experimental.pallas import tpu as pltpu
from jax.sharding import PartitionSpec as P

DOF = 96
DIRS = 9
RHS = 128
NX = 8
NY = 2
NYX = NX * NY
APPLIES = 4
CHUNK = 2
CHUNKS = NYX // CHUNK

FACES = 4


def kernel(src, links_hbm, out, links, vecs, faces, summed, load_sem, send_sem, recv_sem, out_sem):
    t, z = lax.axis_index("ta"), lax.axis_index("gz")
    nt, nz = lax.axis_size("ta"), lax.axis_size("gz")
    t_up, t_down = lax.rem(t + 1, nt), lax.rem(t + nt - 1, nt)
    z_up, z_down = lax.rem(z + 1, nz), lax.rem(z + nz - 1, nz)
    targets = [(t, z_down), (t, z_up), (t_down, z), (t_up, z)]

    load_links = pltpu.make_async_copy(links_hbm, links, load_sem.at[0])
    load_source = pltpu.make_async_copy(src, vecs.at[0], load_sem.at[1])
    load_source.start()
    load_links.start()

    barrier = pltpu.get_barrier_semaphore()
    for target in targets:
        pl.semaphore_signal(barrier, inc=1, device_id=target, device_id_type=pl.DeviceIdType.MESH)
    pl.semaphore_wait(barrier, FACES)

    def push(block, k, c, face):
        return pltpu.make_async_remote_copy(
            src_ref=block,
            dst_ref=faces.at[k, face, pl.ds(c * CHUNK, CHUNK)],
            send_sem=send_sem.at[k, face],
            recv_sem=recv_sem.at[k, face, c],
            device_id=targets[face],
            device_id_type=pl.DeviceIdType.MESH,
        )

    for c in range(CHUNKS):
        for face in range(FACES):
            push(src.at[pl.ds(c * CHUNK, CHUNK)], 0, c, face).start()
    load_source.wait()
    load_links.wait()

    def applied(k, s):
        row, x = s // NX, lax.rem(s, NX)
        here = [
            s,
            row * NX + lax.rem(x + 1, NX),
            row * NX + lax.rem(x + NX - 1, NX),
            lax.rem(s + NX, NYX),
            lax.rem(s + NX, NYX),
        ]
        total = jnp.zeros((DOF, RHS), jnp.float32)
        for d, at in enumerate(here):
            total += jnp.dot(links[s, d], vecs[k, at], preferred_element_type=jnp.float32)
        for face in range(FACES):
            total += jnp.dot(links[s, 5 + face], faces[k, face, s], preferred_element_type=jnp.float32)
        return total

    def arrived(k, c):
        for face in range(FACES):
            push(vecs.at[k, pl.ds(c * CHUNK, CHUNK)], k, c, face).wait_recv()

    def sent(k):
        for face in range(FACES):
            pltpu.make_async_remote_copy(
                src_ref=vecs.at[k],
                dst_ref=faces.at[k, face],
                send_sem=send_sem.at[k, face],
                recv_sem=recv_sem.at[k, face, 0],
                device_id=targets[face],
                device_id_type=pl.DeviceIdType.MESH,
            ).wait_send()

    @pl.loop(0, (APPLIES - 1) * CHUNKS)
    def _(step):
        k, c = step // CHUNKS, lax.rem(step, CHUNKS)
        arrived(k, c)
        for i in range(CHUNK):
            s = c * CHUNK + i
            vecs[k + 1, s] = applied(k, s).astype(jnp.bfloat16)
        for face in range(FACES):
            push(vecs.at[k + 1, pl.ds(c * CHUNK, CHUNK)], k + 1, c, face).start()

    def store(c):
        part = pl.ds(c * CHUNK, CHUNK)
        return pltpu.make_async_copy(summed.at[part], out.at[part], out_sem.at[c])

    @pl.loop(0, CHUNKS)
    def _(c):
        arrived(APPLIES - 1, c)
        for i in range(CHUNK):
            s = c * CHUNK + i
            summed[s] = applied(APPLIES - 1, s)
        store(c).start()

    for k in range(APPLIES):
        sent(k)
    for c in range(CHUNKS):
        store(c).wait()


def shards(source, link_blocks):
    src = source.reshape(NYX, DOF, RHS)
    links = link_blocks.reshape(NYX, DIRS, DOF, DOF)
    total = pl.pallas_call(
        kernel,
        out_shape=jax.ShapeDtypeStruct((NYX, DOF, RHS), jnp.float32),
        in_specs=[pl.BlockSpec(memory_space=pl.ANY)] * 2,
        out_specs=pl.BlockSpec(memory_space=pl.ANY),
        scratch_shapes=[
            pltpu.VMEM((NYX, DIRS, DOF, DOF), jnp.bfloat16),
            pltpu.VMEM((APPLIES, NYX, DOF, RHS), jnp.bfloat16),
            pltpu.VMEM((APPLIES, FACES, NYX, DOF, RHS), jnp.bfloat16),
            pltpu.VMEM((NYX, DOF, RHS), jnp.float32),
            pltpu.SemaphoreType.DMA((2,)),
            pltpu.SemaphoreType.DMA((APPLIES, FACES)),
            pltpu.SemaphoreType.DMA((APPLIES, FACES, CHUNKS)),
            pltpu.SemaphoreType.DMA((CHUNKS,)),
        ],
        compiler_params=pltpu.CompilerParams(
            collective_id=0, has_side_effects=True, vmem_limit_bytes=56 * 2**20
        ),
        cost_estimate=pl.CostEstimate(
            flops=2 * APPLIES * NYX * DIRS * DOF * DOF * RHS, bytes_accessed=6 * 2**20, transcendentals=0
        ),
    )(src, links)
    return total.reshape(1, 1, NYX, DOF, RHS)


def solution(mesh):
    placed = (P("ta", "gz", None, None, None), P("ta", "gz", None, None, None, None))
    return jax.shard_map(
        shards,
        mesh=mesh,
        in_specs=placed,
        out_specs=P("ta", "gz", None, None, None),
        check_vma=False,
    )
```

time: 117 us -> 99.4 us (0.85)
  Pallas kernels: 0 us -> 96.6 us
  waiting for transfers between devices: 71.6 us -> 0 us
  starting transfers between devices: 30.7 us -> 0 us
  matrix products: 10 us -> 0 us
  local copies, waits for them, and re-layouts: 3.41 us -> 2.07 us
    pallas_call x0 -> x1, Pallas kernels: none -> 96.6 us  [shards(): pl.pallas_call(kernel, out_shape=jax.ShapeDtypeStruct((NYX, DOF, RHS), jn...]
    ppermute x16 -> x0, waiting for transfers between devices: 71.6 us -> none  [the longest x8 50.2 us: shifted(): return lax.ppermute(block, axis, route)]
    ppermute x16 -> x0, starting transfers between devices: 30.7 us -> none  [the longest x4 16.8 us: padded(): after = lax.ppermute(first, axis, down)]
    dot_general x36 -> x0, matrix products: 10 us -> none  [apply_operator(): jnp.einsum('tzsab,tzsbr->tzsar', coupling[:, :, :, direction], neighbours...]
    slice x12 -> x0, local copies, waits for them, and re-layouts: 3.4 us -> none  [the longest x8 2.27 us: apply_operator(): jnp.roll(planes, 1, axis=3)]
    unnamed x4 -> x1, local copies, waits for them, and re-layouts: 0.01 us -> 2.07 us
  transfers between devices with their start and end apart: 16 -> 0, of which waited for: 11 -> 0; matrix products, arithmetic and copies ran while one was open for 9% -> 0% of each run, Pallas kernels for 0% -> 0%
where the time goes in v1:
time: 99.4 us; the launch traced here: 98.7 us
  Pallas kernels  96.6 us (97%)
  local copies, waits for them, and re-layouts  2.07 us (2%)
    pallas_call x1, Pallas kernels, shards(): pl.pallas_call(kernel, out_shape=jax.ShapeDtypeStruct((NYX, DOF, RHS), jn...  96.6 us
    unnamed x1, local copies, waits for them, and re-layouts  2.07 us

profile of v1, /device:TPU:25, one launch (start us, length us, event | category | flops | bytes accessed | tf_op | source)
XLA Modules:
  0.0 98.7 jit_solution(18282483618687290330)
XLA Ops:
  0.0 96.6 %shard_map.28 = f32[16,96,128]{2,1,0:T(8,128)} custom-call(bf16[16,96,128]{2,1,0:T(8,128)(2,1)} %bitcast.5, bf16[16,9,96,96]{3,2,1,0:T(8,128)(2,1)} %bitcast.4), custom_call_target="tpu_custom_call" | custom-call | flops 1358954496 | bytes 6291456 | tf_op jit(solution)/shard_map/pallas_call | solution.py:118
  96.6 2.1 %copy.4 = f32[1,1,16,96,128]{4,3,2,1,0:T(8,128)} copy(f32[1,1,16,96,128]{4,3,2,1,0:T(8,128)} %bitcast.3) | data formatting | bytes 1572864

commit v2 on v1

v2 whole, which is shorter than its diff:
```python
import jax
import jax.numpy as jnp
from jax import lax
from jax.experimental import pallas as pl
from jax.experimental.pallas import tpu as pltpu
from jax.sharding import PartitionSpec as P

DOF = 96
DIRS = 9
RHS = 128
NX = 8
NY = 2
NYX = NX * NY
APPLIES = 4
CHUNK = 2
CHUNKS = NYX // CHUNK
STEPS = APPLIES * CHUNKS
DIRECT = CHUNKS
RELAY = CHUNKS
PASS = 4

FACES = 4
MESH = pl.DeviceIdType.MESH


def kernel(src, links_hbm, out, links, vecs, faces, relayed, summed, load_sem, send_sem, recv_sem, relay_sem, pass_sem, out_sem):
    t, z = lax.axis_index("ta"), lax.axis_index("gz")
    nt, nz = lax.axis_size("ta"), lax.axis_size("gz")
    half = nt // 2
    edge = lax.rem(t + 1, half) < 2
    high = t // half
    last = lax.rem(t, half) // (half - 1)
    partner = lax.rem(t + half, nt)

    z_out, z_out_face = lax.rem(z + high + (1 - high) * (nz - 1), nz), high
    z_over, z_over_face = lax.rem(z + (1 - high) + high * (nz - 1), nz), 1 - high
    t_in, t_in_face = lax.rem(t + (1 - last) + last * (nt - 1), nt), 3 - last
    t_over, t_over_face = lax.rem(t + last + (1 - last) * (nt - 1), nt), 2 + last
    t_pass = lax.rem(t_over + half, nt)

    load_links = pltpu.make_async_copy(links_hbm, links, load_sem.at[0])
    load_source = pltpu.make_async_copy(src, vecs.at[0], load_sem.at[1])
    load_source.start()
    load_links.start()

    barrier = pltpu.get_barrier_semaphore()

    def greet(target):
        pl.semaphore_signal(barrier, inc=1, device_id=target, device_id_type=MESH)

    greet((t, z_out))
    greet((t_in, z))
    greet((t, z_over))

    @pl.when(edge)
    def _():
        greet((partner, z))
        greet((partner, z_out))
        greet((t_pass, z))
        pl.semaphore_wait(barrier, 6)

    @pl.when(jnp.logical_not(edge))
    def _():
        greet((t_over, z))
        pl.semaphore_wait(barrier, 4)

    def remote(block, slot, send, recv, target):
        return pltpu.make_async_remote_copy(
            src_ref=block, dst_ref=slot, send_sem=send, recv_sem=recv, device_id=target, device_id_type=MESH
        )

    def part(c):
        return pl.ds(c * CHUNK, CHUNK)

    def push(block, k, c, face, target):
        remote(block, faces.at[k, face, part(c)], send_sem.at[k, face], recv_sem.at[k, face, c], target).start()

    def issue_relay(block, k, c):
        @pl.when(edge)
        def _():
            remote(
                block, relayed.at[k, part(c)], send_sem.at[k, z_over_face], relay_sem.at[k, c], (partner, z)
            ).start()

    def issue_direct(block, k, c):
        push(block, k, c, z_out_face, (t, z_out))

        @pl.when(jnp.logical_not(edge))
        def _():
            push(block, k, c, z_over_face, (t, z_over))
            push(block, k, c, t_over_face, (t_over, z))

        push(block, k, c, t_in_face, (t_in, z))

    def passed(k, c):
        block = relayed.at[k, part(c)]
        on_z = remote(
            block, faces.at[k, z_out_face, part(c)], pass_sem.at[k, 0], recv_sem.at[k, z_out_face, c], (partner, z_out)
        )
        on_t = remote(
            block, faces.at[k, t_over_face, part(c)], pass_sem.at[k, 1], recv_sem.at[k, t_over_face, c], (t_pass, z)
        )
        return on_z, on_t

    def issue_pass(k, c):
        @pl.when(edge)
        def _():
            remote(
                vecs.at[k, part(c)], relayed.at[k, part(c)], send_sem.at[k, 0], relay_sem.at[k, c], (partner, z)
            ).wait_recv()
            on_z, on_t = passed(k, c)
            on_z.start()
            on_t.start()

    def arrived(k, c):
        for face in range(FACES):
            remote(
                vecs.at[k, part(c)], faces.at[k, face, part(c)], send_sem.at[k, face], recv_sem.at[k, face, c], (t_in, z)
            ).wait_recv()

    def applied(k, s):
        row, x = s // NX, lax.rem(s, NX)
        here = [
            s,
            row * NX + lax.rem(x + 1, NX),
            row * NX + lax.rem(x + NX - 1, NX),
            lax.rem(s + NX, NYX),
            lax.rem(s + NX, NYX),
        ]
        total = jnp.zeros((DOF, RHS), jnp.float32)
        for d, at in enumerate(here):
            total += jnp.dot(links[s, d], vecs[k, at], preferred_element_type=jnp.float32)
        for face in range(FACES):
            total += jnp.dot(links[s, 5 + face], faces[k, face, s], preferred_element_type=jnp.float32)
        return total

    def whose(step):
        return step // CHUNKS, lax.rem(step, CHUNKS)

    def direct_at(step):
        k, c = whose(step)
        issue_direct(vecs.at[k, part(c)], k, c)

    def relay_at(step):
        k, c = whose(step)
        issue_relay(vecs.at[k, part(c)], k, c)

    for c in range(RELAY):
        issue_relay(src.at[part(c)], 0, c)
        if c < PASS:
            issue_direct(src.at[part(c)], 0, c)
    for c in range(PASS):
        issue_pass(0, c)
    for c in range(PASS, DIRECT):
        issue_direct(src.at[part(c)], 0, c)
    load_source.wait()
    load_links.wait()

    @pl.loop(0, STEPS - CHUNKS)
    def _(step):
        k, c = whose(step)
        arrived(k, c)
        for i in range(CHUNK):
            s = c * CHUNK + i
            vecs[k + 1, s] = applied(k, s).astype(jnp.bfloat16)
        relay_at(step + RELAY)
        issue_pass(*whose(step + PASS))
        direct_at(step + DIRECT)

    def store(c):
        return pltpu.make_async_copy(summed.at[part(c)], out.at[part(c)], out_sem.at[c])

    @pl.loop(0, CHUNKS)
    def _(c):
        arrived(APPLIES - 1, c)

        @pl.when(c + PASS < CHUNKS)
        def _():
            issue_pass(APPLIES - 1, c + PASS)

        for i in range(CHUNK):
            s = c * CHUNK + i
            summed[s] = applied(APPLIES - 1, s)
        store(c).start()

    def sent(k, sem):
        remote(vecs.at[k], faces.at[k, 0], sem, recv_sem.at[k, 0, 0], (t_in, z)).wait_send()

    for k in range(APPLIES):
        sent(k, send_sem.at[k, z_out_face])
        sent(k, send_sem.at[k, z_over_face])
        sent(k, send_sem.at[k, t_in_face])

        @pl.when(edge)
        def _():
            sent(k, pass_sem.at[k, 0])
            sent(k, pass_sem.at[k, 1])

        @pl.when(jnp.logical_not(edge))
        def _():
            sent(k, send_sem.at[k, t_over_face])

    for c in range(CHUNKS):
        store(c).wait()


def shards(source, link_blocks):
    src = source.reshape(NYX, DOF, RHS)
    links = link_blocks.reshape(NYX, DIRS, DOF, DOF)
    total = pl.pallas_call(
        kernel,
        out_shape=jax.ShapeDtypeStruct((NYX, DOF, RHS), jnp.float32),
        in_specs=[pl.BlockSpec(memory_space=pl.ANY)] * 2,
        out_specs=pl.BlockSpec(memory_space=pl.ANY),
        scratch_shapes=[
            pltpu.VMEM((NYX, DIRS, DOF, DOF), jnp.bfloat16),
            pltpu.VMEM((APPLIES, NYX, DOF, RHS), jnp.bfloat16),
            pltpu.VMEM((APPLIES, FACES, NYX, DOF, RHS), jnp.bfloat16),
            pltpu.VMEM((APPLIES, NYX, DOF, RHS), jnp.bfloat16),
            pltpu.VMEM((NYX, DOF, RHS), jnp.float32),
            pltpu.SemaphoreType.DMA((2,)),
            pltpu.SemaphoreType.DMA((APPLIES, FACES)),
            pltpu.SemaphoreType.DMA((APPLIES, FACES, CHUNKS)),
            pltpu.SemaphoreType.DMA((APPLIES, CHUNKS)),
            pltpu.SemaphoreType.DMA((APPLIES, 2)),
            pltpu.SemaphoreType.DMA((CHUNKS,)),
        ],
        compiler_params=pltpu.CompilerParams(
            collective_id=0, has_side_effects=True, vmem_limit_bytes=56 * 2**20
        ),
        cost_estimate=pl.CostEstimate(
            flops=2 * APPLIES * NYX * DIRS * DOF * DOF * RHS, bytes_accessed=6 * 2**20, transcendentals=0
        ),
    )(src, links)
    return total.reshape(1, 1, NYX, DOF, RHS)


def solution(mesh):
    placed = (P("ta", "gz", None, None, None), P("ta", "gz", None, None, None, None))
    return jax.shard_map(
        shards,
        mesh=mesh,
        in_specs=placed,
        out_specs=P("ta", "gz", None, None, None),
        check_vma=False,
    )
```

time: 99.4 us -> 86.1 us (0.87)
  Pallas kernels: 96.6 us -> 83.3 us
    pallas_call x1, Pallas kernels: 96.6 us -> 83.3 us  [shards(): pl.pallas_call(kernel, out_shape=jax.ShapeDtypeStruct((NYX, DOF, RHS), jn...]
where the time goes in v2:
time: 86.1 us; the launch traced here: 85.4 us
  Pallas kernels  83.3 us (97%)
  local copies, waits for them, and re-layouts  2.07 us (2%)
    pallas_call x1, Pallas kernels, shards(): pl.pallas_call(kernel, out_shape=jax.ShapeDtypeStruct((NYX, DOF, RHS), jn...  83.3 us
    unnamed x1, local copies, waits for them, and re-layouts  2.07 us

profile of v2, /device:TPU:25, one launch (start us, length us, event | category | flops | bytes accessed | tf_op | source)
XLA Modules:
  0.0 85.4 jit_solution(1796982436483722905)
XLA Ops:
  0.0 83.3 %shard_map.28 = f32[16,96,128]{2,1,0:T(8,128)} custom-call(bf16[16,96,128]{2,1,0:T(8,128)(2,1)} %bitcast.5, bf16[16,9,96,96]{3,2,1,0:T(8,128)(2,1)} %bitcast.4), custom_call_target="tpu_custom_call" | custom-call | flops 1358954496 | bytes 6291456 | tf_op jit(solution)/shard_map/pallas_call | solution.py:210
  83.3 2.1 %copy.4 = f32[1,1,16,96,128]{4,3,2,1,0:T(8,128)} copy(f32[1,1,16,96,128]{4,3,2,1,0:T(8,128)} %bitcast.3) | data formatting | bytes 1572864

commit v3 on v2

--- a/solution.py
+++ b/solution.py
@@ -16,8 +16,9 @@
 CHUNKS = NYX // CHUNK
 STEPS = APPLIES * CHUNKS
 DIRECT = CHUNKS
+DIRECT_EDGE = 5
 RELAY = CHUNKS
-PASS = 4
+PASS = 5
 
 FACES = 4
 MESH = pl.DeviceIdType.MESH
@@ -82,15 +83,19 @@
                 block, relayed.at[k, part(c)], send_sem.at[k, z_over_face], relay_sem.at[k, c], (partner, z)
             ).start()
 
-    def issue_direct(block, k, c):
-        push(block, k, c, z_out_face, (t, z_out))
-
+    def issue_edge(block, k, c):
+        @pl.when(edge)
+        def _():
+            push(block, k, c, z_out_face, (t, z_out))
+            push(block, k, c, t_in_face, (t_in, z))
+
+    def issue_inner(block, k, c):
         @pl.when(jnp.logical_not(edge))
         def _():
+            push(block, k, c, z_out_face, (t, z_out))
             push(block, k, c, z_over_face, (t, z_over))
             push(block, k, c, t_over_face, (t_over, z))
-
-        push(block, k, c, t_in_face, (t_in, z))
+            push(block, k, c, t_in_face, (t_in, z))
 
     def passed(k, c):
         block = relayed.at[k, part(c)]
@@ -137,22 +142,17 @@
     def whose(step):
         return step // CHUNKS, lax.rem(step, CHUNKS)
 
-    def direct_at(step):
+    def send(issue, step):
         k, c = whose(step)
-        issue_direct(vecs.at[k, part(c)], k, c)
-
-    def relay_at(step):
-        k, c = whose(step)
-        issue_relay(vecs.at[k, part(c)], k, c)
-
-    for c in range(RELAY):
+        issue(vecs.at[k, part(c)], k, c)
+
+    for c in range(CHUNKS):
         issue_relay(src.at[part(c)], 0, c)
-        if c < PASS:
-            issue_direct(src.at[part(c)], 0, c)
-    for c in range(PASS):
-        issue_pass(0, c)
-    for c in range(PASS, DIRECT):
-        issue_direct(src.at[part(c)], 0, c)
+        issue_inner(src.at[part(c)], 0, c)
+        if c < DIRECT_EDGE:
+            issue_edge(src.at[part(c)], 0, c)
+        if c >= CHUNKS - PASS:
+            issue_pass(0, c - (CHUNKS - PASS))
     load_source.wait()
     load_links.wait()
 
@@ -160,12 +160,13 @@
     def _(step):
         k, c = whose(step)
         arrived(k, c)
+        send(issue_edge, step + DIRECT_EDGE)
         for i in range(CHUNK):
             s = c * CHUNK + i
             vecs[k + 1, s] = applied(k, s).astype(jnp.bfloat16)
-        relay_at(step + RELAY)
+        send(issue_relay, step + RELAY)
+        send(issue_inner, step + DIRECT)
         issue_pass(*whose(step + PASS))
-        direct_at(step + DIRECT)
 
     def store(c):
         return pltpu.make_async_copy(summed.at[part(c)], out.at[part(c)], out_sem.at[c])
@@ -173,6 +174,10 @@
     @pl.loop(0, CHUNKS)
     def _(c):
         arrived(APPLIES - 1, c)
+
+        @pl.when(c + DIRECT_EDGE < CHUNKS)
+        def _():
+            send(issue_edge, STEPS - CHUNKS + c + DIRECT_EDGE)
 
         @pl.when(c + PASS < CHUNKS)
         def _():
@@ -205,8 +210,8 @@
 
 
 def shards(source, link_blocks):
-    src = source.reshape(NYX, DOF, RHS)
-    links = link_blocks.reshape(NYX, DIRS, DOF, DOF)
+    src = pltpu.with_memory_space_constraint(source.reshape(NYX, DOF, RHS), pltpu.HBM)
+    links = pltpu.with_memory_space_constraint(link_blocks.reshape(NYX, DIRS, DOF, DOF), pltpu.HBM)
     total = pl.pallas_call(
         kernel,
         out_shape=jax.ShapeDtypeStruct((NYX, DOF, RHS), jnp.float32),
@@ -226,7 +231,7 @@
             pltpu.SemaphoreType.DMA((CHUNKS,)),
         ],
         compiler_params=pltpu.CompilerParams(
-            collective_id=0, has_side_effects=True, vmem_limit_bytes=56 * 2**20
+            collective_id=0, has_side_effects=True, vmem_limit_bytes=40 * 2**20
         ),
         cost_estimate=pl.CostEstimate(
             flops=2 * APPLIES * NYX * DIRS * DOF * DOF * RHS, bytes_accessed=6 * 2**20, transcendentals=0

time: 86.1 us -> 83.5 us (0.970)
  Pallas kernels: 83.3 us -> 81.4 us
  local copies, waits for them, and re-layouts: 2.07 us -> 0.88 us
    pallas_call x1, Pallas kernels: 83.3 us -> 81.4 us  [shards(): pl.pallas_call(kernel, out_shape=jax.ShapeDtypeStruct((NYX, DOF, RHS), jn...]
    unnamed x1, local copies, waits for them, and re-layouts: 2.07 us -> 0.88 us
where the time goes in v3:
time: 83.5 us; the launch traced here: 82.3 us
  Pallas kernels  81.4 us (97%)
  local copies, waits for them, and re-layouts  0.88 us (1%)
    pallas_call x1, Pallas kernels, shards(): pl.pallas_call(kernel, out_shape=jax.ShapeDtypeStruct((NYX, DOF, RHS), jn...  81.4 us

profile of v3, /device:TPU:25, one launch (start us, length us, event | category | flops | bytes accessed | tf_op | source)
XLA Modules:
  0.0 82.3 jit_solution(12771645427810913992)
XLA Ops:
  0.0 81.4 %shard_map.28 = f32[16,96,128]{2,1,0:T(8,128)S(1)} custom-call(bf16[16,96,128]{2,1,0:T(8,128)(2,1)} %bitcast.5, bf16[16,9,96,96]{3,2,1,0:T(8,128)(2,1)} %bitcast.4), custom_call_target="tpu_custom_call" | custom-call | flops 1358954496 | bytes 6291456 | tf_op jit(solution)/shard_map/pallas_call | solution.py:215
  81.4 0.9 %copy.4 = f32[1,1,16,96,128]{4,3,2,1,0:T(8,128)} copy(f32[1,1,16,96,128]{4,3,2,1,0:T(8,128)S(1)} %bitcast.3) | data formatting | bytes 1572864

commit v4 on v3

--- a/solution.py
+++ b/solution.py
@@ -12,13 +12,14 @@
 NY = 2
 NYX = NX * NY
 APPLIES = 4
-CHUNK = 2
+CHUNK = 1
 CHUNKS = NYX // CHUNK
 STEPS = APPLIES * CHUNKS
-DIRECT = CHUNKS
-DIRECT_EDGE = 5
+DIRECT = 13
+DIRECT_EDGE = 10
 RELAY = CHUNKS
 PASS = 5
+FIRST = 3
 
 FACES = 4
 MESH = pl.DeviceIdType.MESH
@@ -148,11 +149,12 @@
 
     for c in range(CHUNKS):
         issue_relay(src.at[part(c)], 0, c)
-        issue_inner(src.at[part(c)], 0, c)
+        if c < DIRECT:
+            issue_inner(src.at[part(c)], 0, c)
         if c < DIRECT_EDGE:
             issue_edge(src.at[part(c)], 0, c)
-        if c >= CHUNKS - PASS:
-            issue_pass(0, c - (CHUNKS - PASS))
+        if FIRST <= c < FIRST + PASS:
+            issue_pass(0, c - FIRST)
     load_source.wait()
     load_links.wait()
 
@@ -161,11 +163,11 @@
         k, c = whose(step)
         arrived(k, c)
         send(issue_edge, step + DIRECT_EDGE)
+        send(issue_inner, step + DIRECT)
         for i in range(CHUNK):
             s = c * CHUNK + i
             vecs[k + 1, s] = applied(k, s).astype(jnp.bfloat16)
         send(issue_relay, step + RELAY)
-        send(issue_inner, step + DIRECT)
         issue_pass(*whose(step + PASS))
 
     def store(c):
@@ -178,6 +180,10 @@
         @pl.when(c + DIRECT_EDGE < CHUNKS)
         def _():
             send(issue_edge, STEPS - CHUNKS + c + DIRECT_EDGE)
+
+        @pl.when(c + DIRECT < CHUNKS)
+        def _():
+            send(issue_inner, STEPS - CHUNKS + c + DIRECT)
 
         @pl.when(c + PASS < CHUNKS)
         def _():

time: 83.5 us -> 90.1 us (1.079)
  Pallas kernels: 81.4 us -> 88.4 us
    pallas_call x1, Pallas kernels: 81.4 us -> 88.4 us  [shards(): pl.pallas_call(kernel, out_shape=jax.ShapeDtypeStruct((NYX, DOF, RHS), jn...]
where the time goes in v4:
time: 90.1 us; the launch traced here: 89.3 us
  Pallas kernels  88.4 us (98%)
    pallas_call x1, Pallas kernels, shards(): pl.pallas_call(kernel, out_shape=jax.ShapeDtypeStruct((NYX, DOF, RHS), jn...  88.4 us

profile of v4, /device:TPU:25, one launch (start us, length us, event | category | flops | bytes accessed | tf_op | source)
XLA Modules:
  0.0 89.3 jit_solution(560105105317357404)
XLA Ops:
  0.0 88.4 %shard_map.28 = f32[16,96,128]{2,1,0:T(8,128)S(1)} custom-call(bf16[16,96,128]{2,1,0:T(8,128)(2,1)} %bitcast.5, bf16[16,9,96,96]{3,2,1,0:T(8,128)(2,1)} %bitcast.4), custom_call_target="tpu_custom_call" | custom-call | flops 1358954496 | bytes 6291456 | tf_op jit(solution)/shard_map/pallas_call | solution.py:221
  88.4 0.9 copy.4

commit v5 on v3

--- a/solution.py
+++ b/solution.py
@@ -19,6 +19,8 @@
 DIRECT_EDGE = 5
 RELAY = CHUNKS
 PASS = 5
+STRAIGHT = 1
+RELAYED = STEPS - STRAIGHT
 
 FACES = 4
 MESH = pl.DeviceIdType.MESH
@@ -52,17 +54,17 @@
     greet((t, z_out))
     greet((t_in, z))
     greet((t, z_over))
+    greet((t_over, z))
 
     @pl.when(edge)
     def _():
         greet((partner, z))
         greet((partner, z_out))
         greet((t_pass, z))
-        pl.semaphore_wait(barrier, 6)
+        pl.semaphore_wait(barrier, 7)
 
     @pl.when(jnp.logical_not(edge))
     def _():
-        greet((t_over, z))
         pl.semaphore_wait(barrier, 4)
 
     def remote(block, slot, send, recv, target):
@@ -77,7 +79,7 @@
         remote(block, faces.at[k, face, part(c)], send_sem.at[k, face], recv_sem.at[k, face, c], target).start()
 
     def issue_relay(block, k, c):
-        @pl.when(edge)
+        @pl.when(jnp.logical_and(edge, k * CHUNKS + c < RELAYED))
         def _():
             remote(
                 block, relayed.at[k, part(c)], send_sem.at[k, z_over_face], relay_sem.at[k, c], (partner, z)
@@ -88,6 +90,11 @@
         def _():
             push(block, k, c, z_out_face, (t, z_out))
             push(block, k, c, t_in_face, (t_in, z))
+
+        @pl.when(jnp.logical_and(edge, k * CHUNKS + c >= RELAYED))
+        def _():
+            push(block, k, c, z_over_face, (t, z_over))
+            push(block, k, c, t_over_face, (t_over, z))
 
     def issue_inner(block, k, c):
         @pl.when(jnp.logical_not(edge))
@@ -108,7 +115,7 @@
         return on_z, on_t
 
     def issue_pass(k, c):
-        @pl.when(edge)
+        @pl.when(jnp.logical_and(edge, k * CHUNKS + c < RELAYED))
         def _():
             remote(
                 vecs.at[k, part(c)], relayed.at[k, part(c)], send_sem.at[k, 0], relay_sem.at[k, c], (partner, z)
@@ -123,7 +130,7 @@
                 vecs.at[k, part(c)], faces.at[k, face, part(c)], send_sem.at[k, face], recv_sem.at[k, face, c], (t_in, z)
             ).wait_recv()
 
-    def applied(k, s):
+    def at_home(k, s):
         row, x = s // NX, lax.rem(s, NX)
         here = [
             s,
@@ -135,9 +142,16 @@
         total = jnp.zeros((DOF, RHS), jnp.float32)
         for d, at in enumerate(here):
             total += jnp.dot(links[s, d], vecs[k, at], preferred_element_type=jnp.float32)
-        for face in range(FACES):
-            total += jnp.dot(links[s, 5 + face], faces[k, face, s], preferred_element_type=jnp.float32)
         return total
+
+    def applied(k, c, store_site):
+        sites = [c * CHUNK + i for i in range(CHUNK)]
+        totals = [at_home(k, s) for s in sites]
+        arrived(k, c)
+        for s, total in zip(sites, totals):
+            for face in range(FACES):
+                total += jnp.dot(links[s, 5 + face], faces[k, face, s], preferred_element_type=jnp.float32)
+            store_site(s, total)
 
     def whose(step):
         return step // CHUNKS, lax.rem(step, CHUNKS)
@@ -159,11 +173,12 @@
     @pl.loop(0, STEPS - CHUNKS)
     def _(step):
         k, c = whose(step)
-        arrived(k, c)
+
+        def keep(s, total):
+            vecs[k + 1, s] = total.astype(jnp.bfloat16)
+
+        applied(k, c, keep)
         send(issue_edge, step + DIRECT_EDGE)
-        for i in range(CHUNK):
-            s = c * CHUNK + i
-            vecs[k + 1, s] = applied(k, s).astype(jnp.bfloat16)
         send(issue_relay, step + RELAY)
         send(issue_inner, step + DIRECT)
         issue_pass(*whose(step + PASS))
@@ -173,7 +188,10 @@
 
     @pl.loop(0, CHUNKS)
     def _(c):
-        arrived(APPLIES - 1, c)
+        def keep(s, total):
+            summed[s] = total
+
+        applied(APPLIES - 1, c, keep)
 
         @pl.when(c + DIRECT_EDGE < CHUNKS)
         def _():
@@ -183,23 +201,24 @@
         def _():
             issue_pass(APPLIES - 1, c + PASS)
 
-        for i in range(CHUNK):
-            s = c * CHUNK + i
-            summed[s] = applied(APPLIES - 1, s)
         store(c).start()
 
-    def sent(k, sem):
-        remote(vecs.at[k], faces.at[k, 0], sem, recv_sem.at[k, 0, 0], (t_in, z)).wait_send()
+    def sent(k, sem, chunks=CHUNKS):
+        block = pl.ds(0, chunks * CHUNK)
+        remote(vecs.at[k, block], faces.at[k, 0, block], sem, recv_sem.at[k, 0, 0], (t_in, z)).wait_send()
 
     for k in range(APPLIES):
+        straight = STRAIGHT if k == APPLIES - 1 else 0
         sent(k, send_sem.at[k, z_out_face])
         sent(k, send_sem.at[k, z_over_face])
         sent(k, send_sem.at[k, t_in_face])
 
         @pl.when(edge)
         def _():
-            sent(k, pass_sem.at[k, 0])
-            sent(k, pass_sem.at[k, 1])
+            sent(k, pass_sem.at[k, 0], CHUNKS - straight)
+            sent(k, pass_sem.at[k, 1], CHUNKS - straight)
+            if straight:
+                sent(k, send_sem.at[k, t_over_face], straight)
 
         @pl.when(jnp.logical_not(edge))
         def _():

time: 83.5 us -> 84 us (level)
  no operation moved by 1% of the time
where the time goes in v5:
time: 84 us; the launch traced here: 82.4 us
  Pallas kernels  81.5 us (97%)
  local copies, waits for them, and re-layouts  0.88 us (1%)
    pallas_call x1, Pallas kernels, shards(): pl.pallas_call(kernel, out_shape=jax.ShapeDtypeStruct((NYX, DOF, RHS), jn...  81.5 us

profile of v5, /device:TPU:25, one launch (start us, length us, event | category | flops | bytes accessed | tf_op | source)
XLA Modules:
  0.0 82.4 jit_solution(4899567182462862992)
XLA Ops:
  0.0 81.5 %shard_map.28 = f32[16,96,128]{2,1,0:T(8,128)S(1)} custom-call(bf16[16,96,128]{2,1,0:T(8,128)(2,1)} %bitcast.5, bf16[16,9,96,96]{3,2,1,0:T(8,128)(2,1)} %bitcast.4), custom_call_target="tpu_custom_call" | custom-call | flops 1358954496 | bytes 6291456 | tf_op jit(solution)/shard_map/pallas_call | solution.py:234
  81.5 0.9 %copy.4 = f32[1,1,16,96,128]{4,3,2,1,0:T(8,128)} copy(f32[1,1,16,96,128]{4,3,2,1,0:T(8,128)S(1)} %bitcast.3) | data formatting | bytes 1572864

commit v6 on v5

--- a/solution.py
+++ b/solution.py
@@ -17,10 +17,9 @@
 STEPS = APPLIES * CHUNKS
 DIRECT = CHUNKS
 DIRECT_EDGE = 5
+DIRECT_NEAR = 5
 RELAY = CHUNKS
 PASS = 5
-STRAIGHT = 1
-RELAYED = STEPS - STRAIGHT
 
 FACES = 4
 MESH = pl.DeviceIdType.MESH
@@ -31,6 +30,8 @@
     nt, nz = lax.axis_size("ta"), lax.axis_size("gz")
     half = nt // 2
     edge = lax.rem(t + 1, half) < 2
+    near = jnp.logical_and(lax.rem(t + 2, half) < 4, jnp.logical_not(edge))
+    inner = lax.rem(t + 2, half) >= 4
     high = t // half
     last = lax.rem(t, half) // (half - 1)
     partner = lax.rem(t + half, nt)
@@ -54,17 +55,17 @@
     greet((t, z_out))
     greet((t_in, z))
     greet((t, z_over))
-    greet((t_over, z))
 
     @pl.when(edge)
     def _():
         greet((partner, z))
         greet((partner, z_out))
         greet((t_pass, z))
-        pl.semaphore_wait(barrier, 7)
+        pl.semaphore_wait(barrier, 6)
 
     @pl.when(jnp.logical_not(edge))
     def _():
+        greet((t_over, z))
         pl.semaphore_wait(barrier, 4)
 
     def remote(block, slot, send, recv, target):
@@ -79,7 +80,7 @@
         remote(block, faces.at[k, face, part(c)], send_sem.at[k, face], recv_sem.at[k, face, c], target).start()
 
     def issue_relay(block, k, c):
-        @pl.when(jnp.logical_and(edge, k * CHUNKS + c < RELAYED))
+        @pl.when(edge)
         def _():
             remote(
                 block, relayed.at[k, part(c)], send_sem.at[k, z_over_face], relay_sem.at[k, c], (partner, z)
@@ -91,18 +92,21 @@
             push(block, k, c, z_out_face, (t, z_out))
             push(block, k, c, t_in_face, (t_in, z))
 
-        @pl.when(jnp.logical_and(edge, k * CHUNKS + c >= RELAYED))
-        def _():
-            push(block, k, c, z_over_face, (t, z_over))
-            push(block, k, c, t_over_face, (t_over, z))
+    def push_all(block, k, c):
+        push(block, k, c, z_out_face, (t, z_out))
+        push(block, k, c, z_over_face, (t, z_over))
+        push(block, k, c, t_over_face, (t_over, z))
+        push(block, k, c, t_in_face, (t_in, z))
+
+    def issue_near(block, k, c):
+        @pl.when(near)
+        def _():
+            push_all(block, k, c)
 
     def issue_inner(block, k, c):
-        @pl.when(jnp.logical_not(edge))
-        def _():
-            push(block, k, c, z_out_face, (t, z_out))
-            push(block, k, c, z_over_face, (t, z_over))
-            push(block, k, c, t_over_face, (t_over, z))
-            push(block, k, c, t_in_face, (t_in, z))
+        @pl.when(inner)
+        def _():
+            push_all(block, k, c)
 
     def passed(k, c):
         block = relayed.at[k, part(c)]
@@ -115,7 +119,7 @@
         return on_z, on_t
 
     def issue_pass(k, c):
-        @pl.when(jnp.logical_and(edge, k * CHUNKS + c < RELAYED))
+        @pl.when(edge)
         def _():
             remote(
                 vecs.at[k, part(c)], relayed.at[k, part(c)], send_sem.at[k, 0], relay_sem.at[k, c], (partner, z)
@@ -163,6 +167,8 @@
     for c in range(CHUNKS):
         issue_relay(src.at[part(c)], 0, c)
         issue_inner(src.at[part(c)], 0, c)
+        if c < DIRECT_NEAR:
+            issue_near(src.at[part(c)], 0, c)
         if c < DIRECT_EDGE:
             issue_edge(src.at[part(c)], 0, c)
         if c >= CHUNKS - PASS:
@@ -179,9 +185,30 @@
 
         applied(k, c, keep)
         send(issue_edge, step + DIRECT_EDGE)
+        send(issue_near, step + DIRECT_NEAR)
         send(issue_relay, step + RELAY)
         send(issue_inner, step + DIRECT)
         issue_pass(*whose(step + PASS))
+
+    def sent(k, sem):
+        remote(vecs.at[k], faces.at[k, 0], sem, recv_sem.at[k, 0, 0], (t_in, z)).wait_send()
+
+    def sent_round(k):
+        sent(k, send_sem.at[k, z_out_face])
+        sent(k, send_sem.at[k, z_over_face])
+        sent(k, send_sem.at[k, t_in_face])
+
+        @pl.when(edge)
+        def _():
+            sent(k, pass_sem.at[k, 0])
+            sent(k, pass_sem.at[k, 1])
+
+        @pl.when(jnp.logical_not(edge))
+        def _():
+            sent(k, send_sem.at[k, t_over_face])
+
+    for k in range(APPLIES - 2):
+        sent_round(k)
 
     def store(c):
         return pltpu.make_async_copy(summed.at[part(c)], out.at[part(c)], out_sem.at[c])
@@ -192,6 +219,11 @@
             summed[s] = total
 
         applied(APPLIES - 1, c, keep)
+        store(c).start()
+
+        @pl.when(c + DIRECT_NEAR < CHUNKS)
+        def _():
+            send(issue_near, STEPS - CHUNKS + c + DIRECT_NEAR)
 
         @pl.when(c + DIRECT_EDGE < CHUNKS)
         def _():
@@ -201,29 +233,9 @@
         def _():
             issue_pass(APPLIES - 1, c + PASS)
 
-        store(c).start()
-
-    def sent(k, sem, chunks=CHUNKS):
-        block = pl.ds(0, chunks * CHUNK)
-        remote(vecs.at[k, block], faces.at[k, 0, block], sem, recv_sem.at[k, 0, 0], (t_in, z)).wait_send()
-
-    for k in range(APPLIES):
-        straight = STRAIGHT if k == APPLIES - 1 else 0
-        sent(k, send_sem.at[k, z_out_face])
-        sent(k, send_sem.at[k, z_over_face])
-        sent(k, send_sem.at[k, t_in_face])
-
-        @pl.when(edge)
-        def _():
-            sent(k, pass_sem.at[k, 0], CHUNKS - straight)
-            sent(k, pass_sem.at[k, 1], CHUNKS - straight)
-            if straight:
-                sent(k, send_sem.at[k, t_over_face], straight)
-
-        @pl.when(jnp.logical_not(edge))
-        def _():
-            sent(k, send_sem.at[k, t_over_face])
-
+
+    sent_round(APPLIES - 2)
+    sent_round(APPLIES - 1)
     for c in range(CHUNKS):
         store(c).wait()
 

time: 84 us -> 83.4 us (level)
  no operation moved by 1% of the time
where the time goes in v6:
time: 83.4 us; the launch traced here: 82.2 us
  Pallas kernels  81.3 us (97%)
  local copies, waits for them, and re-layouts  0.88 us (1%)
    pallas_call x1, Pallas kernels, shards(): pl.pallas_call(kernel, out_shape=jax.ShapeDtypeStruct((NYX, DOF, RHS), jn...  81.3 us

profile of v6, /device:TPU:25, one launch (start us, length us, event | category | flops | bytes accessed | tf_op | source)
XLA Modules:
  0.0 82.2 jit_solution(10951399519199327562)
XLA Ops:
  0.0 81.3 %shard_map.28 = f32[16,96,128]{2,1,0:T(8,128)S(1)} custom-call(bf16[16,96,128]{2,1,0:T(8,128)(2,1)} %bitcast.5, bf16[16,9,96,96]{3,2,1,0:T(8,128)(2,1)} %bitcast.4), custom_call_target="tpu_custom_call" | custom-call | flops 1358954496 | bytes 6291456 | tf_op jit(solution)/shard_map/pallas_call | solution.py:246
  81.3 0.9 %copy.4 = f32[1,1,16,96,128]{4,3,2,1,0:T(8,128)} copy(f32[1,1,16,96,128]{4,3,2,1,0:T(8,128)S(1)} %bitcast.3) | data formatting | bytes 1572864

commit v7 on v6

--- a/solution.py
+++ b/solution.py
@@ -12,14 +12,15 @@
 NY = 2
 NYX = NX * NY
 APPLIES = 4
-CHUNK = 2
+CHUNK = 1
 CHUNKS = NYX // CHUNK
 STEPS = APPLIES * CHUNKS
 DIRECT = CHUNKS
-DIRECT_EDGE = 5
-DIRECT_NEAR = 5
+DIRECT_EDGE = 10
+DIRECT_NEAR = 13
 RELAY = CHUNKS
-PASS = 5
+PASS = 9
+FIRST = 4
 
 FACES = 4
 MESH = pl.DeviceIdType.MESH
@@ -171,8 +172,8 @@
             issue_near(src.at[part(c)], 0, c)
         if c < DIRECT_EDGE:
             issue_edge(src.at[part(c)], 0, c)
-        if c >= CHUNKS - PASS:
-            issue_pass(0, c - (CHUNKS - PASS))
+        if FIRST <= c < FIRST + PASS:
+            issue_pass(0, c - FIRST)
     load_source.wait()
     load_links.wait()
 

time: 83.4 us -> 86.2 us (1.034)
  the two profiles are of different devices: /device:TPU:25 before, /device:TPU:16 now
where the time goes in v7:
time: 86.2 us
  Pallas kernels  85.3 us (99%)
  local copies, waits for them, and re-layouts  0.88 us (1%)
    pallas_call x1, Pallas kernels, shards(): pl.pallas_call(kernel, out_shape=jax.ShapeDtypeStruct((NYX, DOF, RHS), jn...  85.3 us

profile of v7, /device:TPU:16, one launch (start us, length us, event | category | flops | bytes accessed | tf_op | source)
XLA Modules:
  0.0 86.2 jit_solution(5077873080450534401)
XLA Ops:
  0.0 85.3 %shard_map.28 = f32[16,96,128]{2,1,0:T(8,128)S(1)} custom-call(bf16[16,96,128]{2,1,0:T(8,128)(2,1)} %bitcast.5, bf16[16,9,96,96]{3,2,1,0:T(8,128)(2,1)} %bitcast.4), custom_call_target="tpu_custom_call" | custom-call | flops 1358954496 | bytes 6291456 | tf_op jit(solution)/shard_map/pallas_call | solution.py:247
  85.3 0.9 %copy.4 = f32[1,1,16,96,128]{4,3,2,1,0:T(8,128)} copy(f32[1,1,16,96,128]{4,3,2,1,0:T(8,128)S(1)} %bitcast.3) | data formatting | bytes 1572864

commit v8 on v6

--- a/solution.py
+++ b/solution.py
@@ -22,10 +22,11 @@
 PASS = 5
 
 FACES = 4
+HOME = DIRS - FACES
 MESH = pl.DeviceIdType.MESH
 
 
-def kernel(src, links_hbm, out, links, vecs, faces, relayed, summed, load_sem, send_sem, recv_sem, relay_sem, pass_sem, out_sem):
+def kernel(src, links_hbm, out, links, home_links, face_links, vecs, faces, relayed, summed, load_sem, send_sem, recv_sem, relay_sem, pass_sem, out_sem):
     t, z = lax.axis_index("ta"), lax.axis_index("gz")
     nt, nz = lax.axis_size("ta"), lax.axis_size("gz")
     half = nt // 2
@@ -143,18 +144,16 @@
             lax.rem(s + NX, NYX),
             lax.rem(s + NX, NYX),
         ]
-        total = jnp.zeros((DOF, RHS), jnp.float32)
-        for d, at in enumerate(here):
-            total += jnp.dot(links[s, d], vecs[k, at], preferred_element_type=jnp.float32)
-        return total
+        stacked = jnp.concatenate([vecs[k, at] for at in here], axis=0)
+        return jnp.dot(home_links[s], stacked, preferred_element_type=jnp.float32)
 
     def applied(k, c, store_site):
         sites = [c * CHUNK + i for i in range(CHUNK)]
         totals = [at_home(k, s) for s in sites]
         arrived(k, c)
         for s, total in zip(sites, totals):
-            for face in range(FACES):
-                total += jnp.dot(links[s, 5 + face], faces[k, face, s], preferred_element_type=jnp.float32)
+            stacked = jnp.concatenate([faces[k, face, s] for face in range(FACES)], axis=0)
+            total += jnp.dot(face_links[s], stacked, preferred_element_type=jnp.float32)
             store_site(s, total)
 
     def whose(step):
@@ -176,6 +175,11 @@
     load_source.wait()
     load_links.wait()
 
+    @pl.loop(0, NYX)
+    def _(s):
+        home_links[s] = jnp.concatenate([links[s, d] for d in range(HOME)], axis=1)
+        face_links[s] = jnp.concatenate([links[s, HOME + face] for face in range(FACES)], axis=1)
+
     @pl.loop(0, STEPS - CHUNKS)
     def _(step):
         k, c = whose(step)
@@ -250,6 +254,8 @@
         out_specs=pl.BlockSpec(memory_space=pl.ANY),
         scratch_shapes=[
             pltpu.VMEM((NYX, DIRS, DOF, DOF), jnp.bfloat16),
+            pltpu.VMEM((NYX, DOF, HOME * DOF), jnp.bfloat16),
+            pltpu.VMEM((NYX, DOF, FACES * DOF), jnp.bfloat16),
             pltpu.VMEM((APPLIES, NYX, DOF, RHS), jnp.bfloat16),
             pltpu.VMEM((APPLIES, FACES, NYX, DOF, RHS), jnp.bfloat16),
             pltpu.VMEM((APPLIES, NYX, DOF, RHS), jnp.bfloat16),

time: 83.4 us -> 83.8 us (level)
  no operation moved by 1% of the time
where the time goes in v8:
time: 83.8 us; the launch traced here: 82.3 us
  Pallas kernels  81.4 us (97%)
  local copies, waits for them, and re-layouts  0.88 us (1%)
    pallas_call x1, Pallas kernels, shards(): pl.pallas_call(kernel, out_shape=jax.ShapeDtypeStruct((NYX, DOF, RHS), jn...  81.4 us

profile of v8, /device:TPU:25, one launch (start us, length us, event | category | flops | bytes accessed | tf_op | source)
XLA Modules:
  0.0 82.3 jit_solution(8149117667381151632)
XLA Ops:
  0.0 81.4 %shard_map.28 = f32[16,96,128]{2,1,0:T(8,128)S(1)} custom-call(bf16[16,96,128]{2,1,0:T(8,128)(2,1)} %bitcast.5, bf16[16,9,96,96]{3,2,1,0:T(8,128)(2,1)} %bitcast.4), custom_call_target="tpu_custom_call" | custom-call | flops 1358954496 | bytes 6291456 | tf_op jit(solution)/shard_map/pallas_call | solution.py:250
  81.4 0.9 %copy.4 = f32[1,1,16,96,128]{4,3,2,1,0:T(8,128)} copy(f32[1,1,16,96,128]{4,3,2,1,0:T(8,128)S(1)} %bitcast.3) | data formatting | bytes 1572864

commit v9 on v6

--- a/solution.py
+++ b/solution.py
@@ -15,11 +15,12 @@
 CHUNK = 2
 CHUNKS = NYX // CHUNK
 STEPS = APPLIES * CHUNKS
-DIRECT = CHUNKS
+DIRECT = 6
 DIRECT_EDGE = 5
+DIRECT_STEP = 3
 DIRECT_NEAR = 5
 RELAY = CHUNKS
-PASS = 5
+PASS = 4
 
 FACES = 4
 MESH = pl.DeviceIdType.MESH
@@ -90,6 +91,10 @@
         @pl.when(edge)
         def _():
             push(block, k, c, z_out_face, (t, z_out))
+
+    def issue_edge_in(block, k, c):
+        @pl.when(edge)
+        def _():
             push(block, k, c, t_in_face, (t_in, z))
 
     def push_all(block, k, c):
@@ -164,13 +169,18 @@
         k, c = whose(step)
         issue(vecs.at[k, part(c)], k, c)
 
+    windows = [
+        (issue_inner, DIRECT),
+        (issue_near, DIRECT_NEAR),
+        (issue_edge, DIRECT_EDGE),
+        (issue_edge_in, DIRECT_STEP),
+    ]
+
     for c in range(CHUNKS):
         issue_relay(src.at[part(c)], 0, c)
-        issue_inner(src.at[part(c)], 0, c)
-        if c < DIRECT_NEAR:
-            issue_near(src.at[part(c)], 0, c)
-        if c < DIRECT_EDGE:
-            issue_edge(src.at[part(c)], 0, c)
+        for issue, ahead in windows:
+            if c < ahead:
+                issue(src.at[part(c)], 0, c)
         if c >= CHUNKS - PASS:
             issue_pass(0, c - (CHUNKS - PASS))
     load_source.wait()
@@ -184,10 +194,9 @@
             vecs[k + 1, s] = total.astype(jnp.bfloat16)
 
         applied(k, c, keep)
-        send(issue_edge, step + DIRECT_EDGE)
-        send(issue_near, step + DIRECT_NEAR)
+        for issue, ahead in windows:
+            send(issue, step + ahead)
         send(issue_relay, step + RELAY)
-        send(issue_inner, step + DIRECT)
         issue_pass(*whose(step + PASS))
 
     def sent(k, sem):
@@ -221,13 +230,11 @@
         applied(APPLIES - 1, c, keep)
         store(c).start()
 
-        @pl.when(c + DIRECT_NEAR < CHUNKS)
-        def _():
-            send(issue_near, STEPS - CHUNKS + c + DIRECT_NEAR)
-
-        @pl.when(c + DIRECT_EDGE < CHUNKS)
-        def _():
-            send(issue_edge, STEPS - CHUNKS + c + DIRECT_EDGE)
+        for issue, ahead in windows:
+
+            @pl.when(c + ahead < CHUNKS)
+            def _():
+                send(issue, STEPS - CHUNKS + c + ahead)
 
         @pl.when(c + PASS < CHUNKS)
         def _():

time: 83.4 us -> 84.7 us (1.016)
  Pallas kernels: 81.3 us -> 82.2 us
    pallas_call x1, Pallas kernels: 81.3 us -> 82.2 us  [shards(): pl.pallas_call(kernel, out_shape=jax.ShapeDtypeStruct((NYX, DOF, RHS), jn...]
where the time goes in v9:
time: 84.7 us; the launch traced here: 83.1 us
  Pallas kernels  82.2 us (97%)
  local copies, waits for them, and re-layouts  0.88 us (1%)
    pallas_call x1, Pallas kernels, shards(): pl.pallas_call(kernel, out_shape=jax.ShapeDtypeStruct((NYX, DOF, RHS), jn...  82.2 us

profile of v9, /device:TPU:25, one launch (start us, length us, event | category | flops | bytes accessed | tf_op | source)
XLA Modules:
  0.0 83.1 jit_solution(3796013287311473883)
XLA Ops:
  0.0 82.2 %shard_map.28 = f32[16,96,128]{2,1,0:T(8,128)S(1)} custom-call(bf16[16,96,128]{2,1,0:T(8,128)(2,1)} %bitcast.5, bf16[16,9,96,96]{3,2,1,0:T(8,128)(2,1)} %bitcast.4), custom_call_target="tpu_custom_call" | custom-call | flops 1358954496 | bytes 6291456 | tf_op jit(solution)/shard_map/pallas_call | solution.py:253
  82.2 0.9 %copy.4 = f32[1,1,16,96,128]{4,3,2,1,0:T(8,128)} copy(f32[1,1,16,96,128]{4,3,2,1,0:T(8,128)S(1)} %bitcast.3) | data formatting | bytes 1572864

commit v10 on v9

--- a/solution.py
+++ b/solution.py
@@ -15,12 +15,11 @@
 CHUNK = 2
 CHUNKS = NYX // CHUNK
 STEPS = APPLIES * CHUNKS
+DIRECT_EDGE = 5
+DIRECT_NEAR = 6
 DIRECT = 6
-DIRECT_EDGE = 5
-DIRECT_STEP = 3
-DIRECT_NEAR = 5
 RELAY = CHUNKS
-PASS = 4
+PASS = 5
 
 FACES = 4
 MESH = pl.DeviceIdType.MESH
@@ -31,17 +30,21 @@
     nt, nz = lax.axis_size("ta"), lax.axis_size("gz")
     half = nt // 2
     edge = lax.rem(t + 1, half) < 2
+    off_edge = (lax.rem(t + 1, half) // 2 + half // 2 - 1) // (half // 2)
     near = jnp.logical_and(lax.rem(t + 2, half) < 4, jnp.logical_not(edge))
     inner = lax.rem(t + 2, half) >= 4
     high = t // half
-    last = lax.rem(t, half) // (half - 1)
-    partner = lax.rem(t + half, nt)
+    last = lax.rem(t, half) // (half // 2)
 
     z_out, z_out_face = lax.rem(z + high + (1 - high) * (nz - 1), nz), high
     z_over, z_over_face = lax.rem(z + (1 - high) + high * (nz - 1), nz), 1 - high
     t_in, t_in_face = lax.rem(t + (1 - last) + last * (nt - 1), nt), 3 - last
     t_over, t_over_face = lax.rem(t + last + (1 - last) * (nt - 1), nt), 2 + last
-    t_pass = lax.rem(t_over + half, nt)
+    own_edge = t + off_edge * (2 * last - 1)
+    partner = lax.rem(own_edge + half, nt)
+    partner_near = partner + 1 - 2 * last
+    t_pass = lax.rem(own_edge + last + (1 - last) * (nt - 1) + half, nt)
+    t_pass_near = t_pass - 1 + 2 * last
 
     load_links = pltpu.make_async_copy(links_hbm, links, load_sem.at[0])
     load_source = pltpu.make_async_copy(src, vecs.at[0], load_sem.at[1])
@@ -57,14 +60,25 @@
     greet((t_in, z))
     greet((t, z_over))
 
-    @pl.when(edge)
+    @pl.when(jnp.logical_not(inner))
     def _():
         greet((partner, z))
         greet((partner, z_out))
         greet((t_pass, z))
-        pl.semaphore_wait(barrier, 6)
-
-    @pl.when(jnp.logical_not(edge))
+
+    @pl.when(edge)
+    def _():
+        greet((partner_near, z))
+        greet((partner_near, z_out))
+        greet((t_pass_near, z))
+        pl.semaphore_wait(barrier, 9)
+
+    @pl.when(near)
+    def _():
+        greet((t_over, z))
+        pl.semaphore_wait(barrier, 7)
+
+    @pl.when(inner)
     def _():
         greet((t_over, z))
         pl.semaphore_wait(barrier, 4)
@@ -84,17 +98,17 @@
         @pl.when(edge)
         def _():
             remote(
-                block, relayed.at[k, part(c)], send_sem.at[k, z_over_face], relay_sem.at[k, c], (partner, z)
+                block,
+                relayed.at[k, part(c)],
+                send_sem.at[k, z_over_face],
+                relay_sem.at[k, c],
+                (partner + lax.rem(c, 2) * (partner_near - partner), z),
             ).start()
 
     def issue_edge(block, k, c):
         @pl.when(edge)
         def _():
             push(block, k, c, z_out_face, (t, z_out))
-
-    def issue_edge_in(block, k, c):
-        @pl.when(edge)
-        def _():
             push(block, k, c, t_in_face, (t_in, z))
 
     def push_all(block, k, c):
@@ -124,7 +138,9 @@
         return on_z, on_t
 
     def issue_pass(k, c):
-        @pl.when(edge)
+        odd = lax.rem(c, 2) == 1
+
+        @pl.when(jnp.logical_or(jnp.logical_and(edge, jnp.logical_not(odd)), jnp.logical_and(near, odd)))
         def _():
             remote(
                 vecs.at[k, part(c)], relayed.at[k, part(c)], send_sem.at[k, 0], relay_sem.at[k, c], (partner, z)
@@ -173,16 +189,15 @@
         (issue_inner, DIRECT),
         (issue_near, DIRECT_NEAR),
         (issue_edge, DIRECT_EDGE),
-        (issue_edge_in, DIRECT_STEP),
     ]
 
     for c in range(CHUNKS):
-        issue_relay(src.at[part(c)], 0, c)
+        issue_relay(src.at[part(c)], 0, jnp.int32(c))
         for issue, ahead in windows:
             if c < ahead:
                 issue(src.at[part(c)], 0, c)
         if c >= CHUNKS - PASS:
-            issue_pass(0, c - (CHUNKS - PASS))
+            issue_pass(0, jnp.int32(c - (CHUNKS - PASS)))
     load_source.wait()
     load_links.wait()
 
@@ -199,18 +214,19 @@
         send(issue_relay, step + RELAY)
         issue_pass(*whose(step + PASS))
 
-    def sent(k, sem):
-        remote(vecs.at[k], faces.at[k, 0], sem, recv_sem.at[k, 0, 0], (t_in, z)).wait_send()
+    def sent(k, sem, sites=NYX):
+        block = pl.ds(0, sites)
+        remote(vecs.at[k, block], faces.at[k, 0, block], sem, recv_sem.at[k, 0, 0], (t_in, z)).wait_send()
 
     def sent_round(k):
         sent(k, send_sem.at[k, z_out_face])
         sent(k, send_sem.at[k, z_over_face])
         sent(k, send_sem.at[k, t_in_face])
 
-        @pl.when(edge)
-        def _():
-            sent(k, pass_sem.at[k, 0])
-            sent(k, pass_sem.at[k, 1])
+        @pl.when(jnp.logical_not(inner))
+        def _():
+            sent(k, pass_sem.at[k, 0], NYX // 2)
+            sent(k, pass_sem.at[k, 1], NYX // 2)
 
         @pl.when(jnp.logical_not(edge))
         def _():

time: 84.7 us -> 83.4 us (0.985)
  no operation moved by 1% of the time
where the time goes in v10:
time: 83.4 us; the launch traced here: 82.5 us
  Pallas kernels  81.6 us (98%)
  local copies, waits for them, and re-layouts  0.88 us (1%)
    pallas_call x1, Pallas kernels, shards(): pl.pallas_call(kernel, out_shape=jax.ShapeDtypeStruct((NYX, DOF, RHS), jn...  81.6 us

profile of v10, /device:TPU:25, one launch (start us, length us, event | category | flops | bytes accessed | tf_op | source)
XLA Modules:
  0.0 82.5 jit_solution(11858777220987842950)
XLA Ops:
  0.0 81.6 %shard_map.28 = f32[16,96,128]{2,1,0:T(8,128)S(1)} custom-call(bf16[16,96,128]{2,1,0:T(8,128)(2,1)} %bitcast.5, bf16[16,9,96,96]{3,2,1,0:T(8,128)(2,1)} %bitcast.4), custom_call_target="tpu_custom_call" | custom-call | flops 1358954496 | bytes 6291456 | tf_op jit(solution)/shard_map/pallas_call | solution.py:269
  81.6 0.9 %copy.4 = f32[1,1,16,96,128]{4,3,2,1,0:T(8,128)} copy(f32[1,1,16,96,128]{4,3,2,1,0:T(8,128)S(1)} %bitcast.3) | data formatting | bytes 1572864

commit v11 on v10

--- a/solution.py
+++ b/solution.py
@@ -48,8 +48,6 @@
 
     load_links = pltpu.make_async_copy(links_hbm, links, load_sem.at[0])
     load_source = pltpu.make_async_copy(src, vecs.at[0], load_sem.at[1])
-    load_source.start()
-    load_links.start()
 
     barrier = pltpu.get_barrier_semaphore()
 
@@ -59,6 +57,7 @@
     greet((t, z_out))
     greet((t_in, z))
     greet((t, z_over))
+    load_source.start(priority=1)
 
     @pl.when(jnp.logical_not(inner))
     def _():
@@ -196,6 +195,8 @@
         for issue, ahead in windows:
             if c < ahead:
                 issue(src.at[part(c)], 0, c)
+        if c == 1:
+            load_links.start(priority=1)
         if c >= CHUNKS - PASS:
             issue_pass(0, jnp.int32(c - (CHUNKS - PASS)))
     load_source.wait()

time: 83.4 us -> 83.4 us (level)
  no operation moved by 1% of the time
where the time goes in v11:
time: 83.4 us; the launch traced here: 82.5 us
  Pallas kernels  81.6 us (98%)
  local copies, waits for them, and re-layouts  0.88 us (1%)
    pallas_call x1, Pallas kernels, shards(): pl.pallas_call(kernel, out_shape=jax.ShapeDtypeStruct((NYX, DOF, RHS), jn...  81.6 us

profile of v11, /device:TPU:25, one launch (start us, length us, event | category | flops | bytes accessed | tf_op | source)
XLA Modules:
  0.0 82.5 jit_solution(6791094720573228929)
XLA Ops:
  0.0 81.6 %shard_map.28 = f32[16,96,128]{2,1,0:T(8,128)S(1)} custom-call(bf16[16,96,128]{2,1,0:T(8,128)(2,1)} %bitcast.5, bf16[16,9,96,96]{3,2,1,0:T(8,128)(2,1)} %bitcast.4), custom_call_target="tpu_custom_call" | custom-call | flops 1358954496 | bytes 6291456 | tf_op jit(solution)/shard_map/pallas_call | solution.py:270
  81.6 0.9 %copy.4 = f32[1,1,16,96,128]{4,3,2,1,0:T(8,128)} copy(f32[1,1,16,96,128]{4,3,2,1,0:T(8,128)S(1)} %bitcast.3) | data formatting | bytes 1572864

commit v12 on v10

--- a/solution.py
+++ b/solution.py
@@ -16,10 +16,10 @@
 CHUNKS = NYX // CHUNK
 STEPS = APPLIES * CHUNKS
 DIRECT_EDGE = 5
-DIRECT_NEAR = 6
-DIRECT = 6
+DIRECT_NEAR = CHUNKS
+DIRECT = CHUNKS
 RELAY = CHUNKS
-PASS = 5
+PASS = 4
 
 FACES = 4
 MESH = pl.DeviceIdType.MESH

time: 83.4 us -> 83.8 us (level)
  Pallas kernels: 81.6 us -> 82.8 us
    pallas_call x1, Pallas kernels: 81.6 us -> 82.8 us  [shards(): pl.pallas_call(kernel, out_shape=jax.ShapeDtypeStruct((NYX, DOF, RHS), jn...]
where the time goes in v12:
time: 83.8 us; the launch traced here: 83.7 us
  Pallas kernels  82.8 us (99%)
  local copies, waits for them, and re-layouts  0.88 us (1%)
    pallas_call x1, Pallas kernels, shards(): pl.pallas_call(kernel, out_shape=jax.ShapeDtypeStruct((NYX, DOF, RHS), jn...  82.8 us

profile of v12, /device:TPU:25, one launch (start us, length us, event | category | flops | bytes accessed | tf_op | source)
XLA Modules:
  0.0 83.7 jit_solution(12462403767194375505)
XLA Ops:
  0.0 82.8 %shard_map.28 = f32[16,96,128]{2,1,0:T(8,128)S(1)} custom-call(bf16[16,96,128]{2,1,0:T(8,128)(2,1)} %bitcast.5, bf16[16,9,96,96]{3,2,1,0:T(8,128)(2,1)} %bitcast.4), custom_call_target="tpu_custom_call" | custom-call | flops 1358954496 | bytes 6291456 | tf_op jit(solution)/shard_map/pallas_call | solution.py:269
  82.8 0.9 %copy.4 = f32[1,1,16,96,128]{4,3,2,1,0:T(8,128)} copy(f32[1,1,16,96,128]{4,3,2,1,0:T(8,128)S(1)} %bitcast.3) | data formatting | bytes 1572864

commit v13 on v12

--- a/solution.py
+++ b/solution.py
@@ -15,11 +15,12 @@
 CHUNK = 2
 CHUNKS = NYX // CHUNK
 STEPS = APPLIES * CHUNKS
-DIRECT_EDGE = 5
+DIRECT_EDGE = 3
+DIRECT_EDGE_IN = 7
 DIRECT_NEAR = CHUNKS
 DIRECT = CHUNKS
 RELAY = CHUNKS
-PASS = 4
+PASS = 3
 
 FACES = 4
 MESH = pl.DeviceIdType.MESH
@@ -109,6 +110,10 @@
         @pl.when(edge)
         def _():
             push(block, k, c, z_out_face, (t, z_out))
+
+    def issue_edge_in(block, k, c):
+        @pl.when(edge)
+        def _():
             push(block, k, c, t_in_face, (t_in, z))
 
     def push_all(block, k, c):
@@ -189,6 +194,7 @@
         (issue_inner, DIRECT),
         (issue_near, DIRECT_NEAR),
         (issue_edge, DIRECT_EDGE),
+        (issue_edge_in, DIRECT_EDGE_IN),
     ]
 
     for c in range(CHUNKS):

time: 83.8 us -> 87.2 us (1.041)
  the two profiles are of different devices: /device:TPU:25 before, /device:TPU:32 now
where the time goes in v13:
time: 87.2 us; the launch traced here: 87.1 us
  Pallas kernels  86.3 us (99%)
  local copies, waits for them, and re-layouts  0.88 us (1%)
    pallas_call x1, Pallas kernels, shards(): pl.pallas_call(kernel, out_shape=jax.ShapeDtypeStruct((NYX, DOF, RHS), jn...  86.3 us

profile of v13, /device:TPU:32, one launch (start us, length us, event | category | flops | bytes accessed | tf_op | source)
XLA Modules:
  0.0 87.1 jit_solution(12622676613662510881)
XLA Ops:
  0.0 86.3 %shard_map.28 = f32[16,96,128]{2,1,0:T(8,128)S(1)} custom-call(bf16[16,96,128]{2,1,0:T(8,128)(2,1)} %bitcast.5, bf16[16,9,96,96]{3,2,1,0:T(8,128)(2,1)} %bitcast.4), custom_call_target="tpu_custom_call" | custom-call | flops 1358954496 | bytes 6291456 | tf_op jit(solution)/shard_map/pallas_call | solution.py:275
  86.3 0.9 %copy.4 = f32[1,1,16,96,128]{4,3,2,1,0:T(8,128)} copy(f32[1,1,16,96,128]{4,3,2,1,0:T(8,128)S(1)} %bitcast.3) | data formatting | bytes 1572864

commit v14 on v10

--- a/solution.py
+++ b/solution.py
@@ -15,17 +15,18 @@
 CHUNK = 2
 CHUNKS = NYX // CHUNK
 STEPS = APPLIES * CHUNKS
-DIRECT_EDGE = 5
-DIRECT_NEAR = 6
-DIRECT = 6
+DIRECT_EDGE = 6
+DIRECT_NEAR = 7
+DIRECT = 7
 RELAY = CHUNKS
 PASS = 5
 
 FACES = 4
+HOME = DIRS - FACES
 MESH = pl.DeviceIdType.MESH
 
 
-def kernel(src, links_hbm, out, links, vecs, faces, relayed, summed, load_sem, send_sem, recv_sem, relay_sem, pass_sem, out_sem):
+def kernel(src, links_hbm, out, links, home_links, face_links, vecs, faces, relayed, summed, load_sem, send_sem, recv_sem, relay_sem, pass_sem, out_sem):
     t, z = lax.axis_index("ta"), lax.axis_index("gz")
     nt, nz = lax.axis_size("ta"), lax.axis_size("gz")
     half = nt // 2
@@ -164,18 +165,16 @@
             lax.rem(s + NX, NYX),
             lax.rem(s + NX, NYX),
         ]
-        total = jnp.zeros((DOF, RHS), jnp.float32)
-        for d, at in enumerate(here):
-            total += jnp.dot(links[s, d], vecs[k, at], preferred_element_type=jnp.float32)
-        return total
+        stacked = jnp.concatenate([vecs[k, at] for at in here], axis=0)
+        return jnp.dot(home_links[s], stacked, preferred_element_type=jnp.float32)
 
     def applied(k, c, store_site):
         sites = [c * CHUNK + i for i in range(CHUNK)]
         totals = [at_home(k, s) for s in sites]
         arrived(k, c)
         for s, total in zip(sites, totals):
-            for face in range(FACES):
-                total += jnp.dot(links[s, 5 + face], faces[k, face, s], preferred_element_type=jnp.float32)
+            stacked = jnp.concatenate([faces[k, face, s] for face in range(FACES)], axis=0)
+            total += jnp.dot(face_links[s], stacked, preferred_element_type=jnp.float32)
             store_site(s, total)
 
     def whose(step):
@@ -200,6 +199,11 @@
             issue_pass(0, jnp.int32(c - (CHUNKS - PASS)))
     load_source.wait()
     load_links.wait()
+
+    @pl.loop(0, NYX)
+    def _(s):
+        home_links[s] = jnp.concatenate([links[s, d] for d in range(HOME)], axis=1)
+        face_links[s] = jnp.concatenate([links[s, HOME + face] for face in range(FACES)], axis=1)
 
     @pl.loop(0, STEPS - CHUNKS)
     def _(step):
@@ -273,6 +277,8 @@
         out_specs=pl.BlockSpec(memory_space=pl.ANY),
         scratch_shapes=[
             pltpu.VMEM((NYX, DIRS, DOF, DOF), jnp.bfloat16),
+            pltpu.VMEM((NYX, DOF, HOME * DOF), jnp.bfloat16),
+            pltpu.VMEM((NYX, DOF, FACES * DOF), jnp.bfloat16),
             pltpu.VMEM((APPLIES, NYX, DOF, RHS), jnp.bfloat16),
             pltpu.VMEM((APPLIES, FACES, NYX, DOF, RHS), jnp.bfloat16),
             pltpu.VMEM((APPLIES, NYX, DOF, RHS), jnp.bfloat16),

time: 83.4 us -> 83.5 us (level)
  Pallas kernels: 81.6 us -> 82.5 us
    pallas_call x1, Pallas kernels: 81.6 us -> 82.5 us  [shards(): pl.pallas_call(kernel, out_shape=jax.ShapeDtypeStruct((NYX, DOF, RHS), jn...]
where the time goes in v14:
time: 83.5 us; the launch traced here: 83.4 us
  Pallas kernels  82.5 us (99%)
  local copies, waits for them, and re-layouts  0.88 us (1%)
    pallas_call x1, Pallas kernels, shards(): pl.pallas_call(kernel, out_shape=jax.ShapeDtypeStruct((NYX, DOF, RHS), jn...  82.5 us

profile of v14, /device:TPU:25, one launch (start us, length us, event | category | flops | bytes accessed | tf_op | source)
XLA Modules:
  0.0 83.4 jit_solution(10108262485529422236)
XLA Ops:
  0.0 82.5 %shard_map.28 = f32[16,96,128]{2,1,0:T(8,128)S(1)} custom-call(bf16[16,96,128]{2,1,0:T(8,128)(2,1)} %bitcast.5, bf16[16,9,96,96]{3,2,1,0:T(8,128)(2,1)} %bitcast.4), custom_call_target="tpu_custom_call" | custom-call | flops 1358954496 | bytes 6291456 | tf_op jit(solution)/shard_map/pallas_call | solution.py:273
  82.5 0.9 %copy.4 = f32[1,1,16,96,128]{4,3,2,1,0:T(8,128)} copy(f32[1,1,16,96,128]{4,3,2,1,0:T(8,128)S(1)} %bitcast.3) | data formatting | bytes 1572864

commit v15 on v10

--- a/solution.py
+++ b/solution.py
@@ -15,11 +15,11 @@
 CHUNK = 2
 CHUNKS = NYX // CHUNK
 STEPS = APPLIES * CHUNKS
-DIRECT_EDGE = 5
+DIRECT_EDGE = 6
 DIRECT_NEAR = 6
 DIRECT = 6
 RELAY = CHUNKS
-PASS = 5
+PASS = 3
 
 FACES = 4
 MESH = pl.DeviceIdType.MESH

time: 83.4 us -> 84.8 us (1.017)
  Pallas kernels: 81.6 us -> 83.1 us
    pallas_call x1, Pallas kernels: 81.6 us -> 83.1 us  [shards(): pl.pallas_call(kernel, out_shape=jax.ShapeDtypeStruct((NYX, DOF, RHS), jn...]
where the time goes in v15:
time: 84.8 us; the launch traced here: 84 us
  Pallas kernels  83.1 us (98%)
  local copies, waits for them, and re-layouts  0.88 us (1%)
    pallas_call x1, Pallas kernels, shards(): pl.pallas_call(kernel, out_shape=jax.ShapeDtypeStruct((NYX, DOF, RHS), jn...  83.1 us

profile of v15, /device:TPU:25, one launch (start us, length us, event | category | flops | bytes accessed | tf_op | source)
XLA Modules:
  0.0 84.0 jit_solution(6072297701865101408)
XLA Ops:
  0.0 83.1 %shard_map.28 = f32[16,96,128]{2,1,0:T(8,128)S(1)} custom-call(bf16[16,96,128]{2,1,0:T(8,128)(2,1)} %bitcast.5, bf16[16,9,96,96]{3,2,1,0:T(8,128)(2,1)} %bitcast.4), custom_call_target="tpu_custom_call" | custom-call | flops 1358954496 | bytes 6291456 | tf_op jit(solution)/shard_map/pallas_call | solution.py:269
  83.1 0.9 %copy.4 = f32[1,1,16,96,128]{4,3,2,1,0:T(8,128)} copy(f32[1,1,16,96,128]{4,3,2,1,0:T(8,128)S(1)} %bitcast.3) | data formatting | bytes 1572864

commit v16 on v15

--- a/solution.py
+++ b/solution.py
@@ -19,7 +19,7 @@
 DIRECT_NEAR = 6
 DIRECT = 6
 RELAY = CHUNKS
-PASS = 3
+PASS = 6
 
 FACES = 4
 MESH = pl.DeviceIdType.MESH

time: 84.8 us -> 84 us (level)
  Pallas kernels: 83.1 us -> 81.6 us
    pallas_call x1, Pallas kernels: 83.1 us -> 81.6 us  [shards(): pl.pallas_call(kernel, out_shape=jax.ShapeDtypeStruct((NYX, DOF, RHS), jn...]
where the time goes in v16:
time: 84 us; the launch traced here: 82.5 us
  Pallas kernels  81.6 us (97%)
  local copies, waits for them, and re-layouts  0.88 us (1%)
    pallas_call x1, Pallas kernels, shards(): pl.pallas_call(kernel, out_shape=jax.ShapeDtypeStruct((NYX, DOF, RHS), jn...  81.6 us

profile of v16, /device:TPU:25, one launch (start us, length us, event | category | flops | bytes accessed | tf_op | source)
XLA Modules:
  0.0 82.5 jit_solution(2472367384398695850)
XLA Ops:
  0.0 81.6 %shard_map.28 = f32[16,96,128]{2,1,0:T(8,128)S(1)} custom-call(bf16[16,96,128]{2,1,0:T(8,128)(2,1)} %bitcast.5, bf16[16,9,96,96]{3,2,1,0:T(8,128)(2,1)} %bitcast.4), custom_call_target="tpu_custom_call" | custom-call | flops 1358954496 | bytes 6291456 | tf_op jit(solution)/shard_map/pallas_call | solution.py:269
  81.7 0.9 %copy.4 = f32[1,1,16,96,128]{4,3,2,1,0:T(8,128)} copy(f32[1,1,16,96,128]{4,3,2,1,0:T(8,128)S(1)} %bitcast.3) | data formatting | bytes 1572864

commit v17 on v10

--- a/solution.py
+++ b/solution.py
@@ -25,7 +25,7 @@
 MESH = pl.DeviceIdType.MESH
 
 
-def kernel(src, links_hbm, out, links, vecs, faces, relayed, summed, load_sem, send_sem, recv_sem, relay_sem, pass_sem, out_sem):
+def kernel(src, links_hbm, out, links, vecs, faces, relayed, load_sem, send_sem, recv_sem, relay_sem, pass_sem):
     t, z = lax.axis_index("ta"), lax.axis_index("gz")
     nt, nz = lax.axis_size("ta"), lax.axis_size("gz")
     half = nt // 2
@@ -235,16 +235,12 @@
     for k in range(APPLIES - 2):
         sent_round(k)
 
-    def store(c):
-        return pltpu.make_async_copy(summed.at[part(c)], out.at[part(c)], out_sem.at[c])
-
     @pl.loop(0, CHUNKS)
     def _(c):
         def keep(s, total):
-            summed[s] = total
+            out[s] = total
 
         applied(APPLIES - 1, c, keep)
-        store(c).start()
 
         for issue, ahead in windows:
 
@@ -259,8 +255,6 @@
 
     sent_round(APPLIES - 2)
     sent_round(APPLIES - 1)
-    for c in range(CHUNKS):
-        store(c).wait()
 
 
 def shards(source, link_blocks):
@@ -268,21 +262,19 @@
     links = pltpu.with_memory_space_constraint(link_blocks.reshape(NYX, DIRS, DOF, DOF), pltpu.HBM)
     total = pl.pallas_call(
         kernel,
-        out_shape=jax.ShapeDtypeStruct((NYX, DOF, RHS), jnp.float32),
+        out_shape=pltpu.VMEM((NYX, DOF, RHS), jnp.float32),
         in_specs=[pl.BlockSpec(memory_space=pl.ANY)] * 2,
-        out_specs=pl.BlockSpec(memory_space=pl.ANY),
+        out_specs=pl.BlockSpec(memory_space=pltpu.VMEM),
         scratch_shapes=[
             pltpu.VMEM((NYX, DIRS, DOF, DOF), jnp.bfloat16),
             pltpu.VMEM((APPLIES, NYX, DOF, RHS), jnp.bfloat16),
             pltpu.VMEM((APPLIES, FACES, NYX, DOF, RHS), jnp.bfloat16),
             pltpu.VMEM((APPLIES, NYX, DOF, RHS), jnp.bfloat16),
-            pltpu.VMEM((NYX, DOF, RHS), jnp.float32),
             pltpu.SemaphoreType.DMA((2,)),
             pltpu.SemaphoreType.DMA((APPLIES, FACES)),
             pltpu.SemaphoreType.DMA((APPLIES, FACES, CHUNKS)),
             pltpu.SemaphoreType.DMA((APPLIES, CHUNKS)),
             pltpu.SemaphoreType.DMA((APPLIES, 2)),
-            pltpu.SemaphoreType.DMA((CHUNKS,)),
         ],
         compiler_params=pltpu.CompilerParams(
             collective_id=0, has_side_effects=True, vmem_limit_bytes=40 * 2**20

time: 83.4 us -> 83.1 us (level)
  no operation moved by 1% of the time
where the time goes in v17:
time: 83.1 us; the launch traced here: 82.3 us
  Pallas kernels  81.4 us (98%)
  local copies, waits for them, and re-layouts  0.88 us (1%)
    pallas_call x1, Pallas kernels, shards(): pl.pallas_call(kernel, out_shape=pltpu.VMEM((NYX, DOF, RHS), jnp.float32)...  81.4 us

profile of v17, /device:TPU:25, one launch (start us, length us, event | category | flops | bytes accessed | tf_op | source)
XLA Modules:
  0.0 82.3 jit_solution(5434865951666068595)
XLA Ops:
  0.0 81.4 %shard_map.28 = f32[16,96,128]{2,1,0:T(8,128)S(1)} custom-call(bf16[16,96,128]{2,1,0:T(8,128)(2,1)} %bitcast.5, bf16[16,9,96,96]{3,2,1,0:T(8,128)(2,1)} %bitcast.4), custom_call_target="tpu_custom_call" | custom-call | flops 1358954496 | bytes 6291456 | tf_op jit(solution)/shard_map/pallas_call | solution.py:263
  81.4 0.9 %copy.4 = f32[1,1,16,96,128]{4,3,2,1,0:T(8,128)} copy(f32[1,1,16,96,128]{4,3,2,1,0:T(8,128)S(1)} %bitcast.3) | data formatting | bytes 1572864

commit v18 on v17

--- a/solution.py
+++ b/solution.py
@@ -169,10 +169,11 @@
             total += jnp.dot(links[s, d], vecs[k, at], preferred_element_type=jnp.float32)
         return total
 
-    def applied(k, c, store_site):
+    def applied(k, c, store_site, send_ready):
         sites = [c * CHUNK + i for i in range(CHUNK)]
         totals = [at_home(k, s) for s in sites]
         arrived(k, c)
+        send_ready()
         for s, total in zip(sites, totals):
             for face in range(FACES):
                 total += jnp.dot(links[s, 5 + face], faces[k, face, s], preferred_element_type=jnp.float32)
@@ -208,9 +209,11 @@
         def keep(s, total):
             vecs[k + 1, s] = total.astype(jnp.bfloat16)
 
-        applied(k, c, keep)
-        for issue, ahead in windows:
-            send(issue, step + ahead)
+        def send_ready():
+            for issue, ahead in windows:
+                send(issue, step + ahead)
+
+        applied(k, c, keep, send_ready)
         send(issue_relay, step + RELAY)
         issue_pass(*whose(step + PASS))
 
@@ -240,13 +243,14 @@
         def keep(s, total):
             out[s] = total
 
-        applied(APPLIES - 1, c, keep)
-
-        for issue, ahead in windows:
-
-            @pl.when(c + ahead < CHUNKS)
-            def _():
-                send(issue, STEPS - CHUNKS + c + ahead)
+        def send_ready():
+            for issue, ahead in windows:
+
+                @pl.when(c + ahead < CHUNKS)
+                def _():
+                    send(issue, STEPS - CHUNKS + c + ahead)
+
+        applied(APPLIES - 1, c, keep, send_ready)
 
         @pl.when(c + PASS < CHUNKS)
         def _():

time: 83.1 us -> 83.8 us (level)
  no operation moved by 1% of the time
where the time goes in v18:
time: 83.8 us; the launch traced here: 82.3 us
  Pallas kernels  81.4 us (97%)
  local copies, waits for them, and re-layouts  0.88 us (1%)
    pallas_call x1, Pallas kernels, shards(): pl.pallas_call(kernel, out_shape=pltpu.VMEM((NYX, DOF, RHS), jnp.float32)...  81.4 us

profile of v18, /device:TPU:25, one launch (start us, length us, event | category | flops | bytes accessed | tf_op | source)
XLA Modules:
  0.0 82.3 jit_solution(13469045562672375926)
XLA Ops:
  0.0 81.4 %shard_map.28 = f32[16,96,128]{2,1,0:T(8,128)S(1)} custom-call(bf16[16,96,128]{2,1,0:T(8,128)(2,1)} %bitcast.5, bf16[16,9,96,96]{3,2,1,0:T(8,128)(2,1)} %bitcast.4), custom_call_target="tpu_custom_call" | custom-call | flops 1358954496 | bytes 6291456 | tf_op jit(solution)/shard_map/pallas_call | solution.py:267
  81.4 0.9 %copy.4 = f32[1,1,16,96,128]{4,3,2,1,0:T(8,128)} copy(f32[1,1,16,96,128]{4,3,2,1,0:T(8,128)S(1)} %bitcast.3) | data formatting | bytes 1572864
